TPU v7x, 32 devices: a whole 2x2x4 slice. The times are simulated.
32 devices in a mesh: seq: 4 (over z), dp: 8 (over y, x, core).
Axes of the slice: x: 2, y: 2, z: 4, core: 2. Of those that a mesh axis runs over, the one named last changes fastest.
Arguments:
- layer_input: bfloat16 [8192, 1024], P(('dp', 'seq')), may hold values from -6 to 6
- out_grad: bfloat16 [8192, 1024], P(('dp', 'seq')), may hold values from -6 to 6
- lengths: int32 [8, 3], P('dp'), may hold values from 1 to 682, 1024 in all within a row
- item_owner: int32 [8192, 1], P(('dp', 'seq')), may hold values from 0 to 31; in each aligned block of 256 rows (0 to 255, 256 to 511, ...) at most 16 rows name the same one
- item_row: int32 [8192], P(('dp', 'seq')), may hold values from 0 to 511
- w_attn: bfloat16 [1024, 3072], replicated, may hold values from -0.1875 to 0.1875
- w_gate: bfloat16 [1024, 1024], replicated, may hold values from -0.1875 to 0.1875
- w_out: bfloat16 [1024, 1024], replicated, may hold values from -0.1875 to 0.1875
- emb_table: float32 [16384, 1024], P(('seq', 'dp')), may hold values from -6 to 6
- row_accum: float32 [16384], P(('seq', 'dp')), may hold values from 0.25 to 4
Outputs:
- grad_attn: float32 [1024, 3072], P('dp', 'seq')
- grad_gate: float32 [1024, 1024], P('dp', 'seq')
- grad_out: float32 [1024, 1024], P('dp', 'seq')
- new_table: float32 [16384, 1024], P(('seq', 'dp'))
- new_accum: float32 [16384], P(('seq', 'dp'))
Inputs may be any that keep to these rules, and one draw needn't show every extreme that they name: Each group's 3 lengths sum to 1024; the largest is exactly 682. `item_owner`: among the 256 events of one device at most 16 name one owner, a bound that some block reaches.
All inputs are finite; a program needn't handle non-finite values.
Results may differ from a plain program's by a relative error of at most 0.0092.
Values may be sent and summed in bfloat16 or wider, within the bound.
No kernel may reach another device: no remote copies, remote signals or barrier semaphores. Data moves between devices by JAX's collectives and lax.ppermute only.
A program may use at most 128 MiB of HBM per device.

v0:
```python
import functools

import jax
import jax.numpy as jnp
from jax import lax
from jax.experimental import pallas as pl
from jax.experimental.pallas import tpu as pltpu
from jax.sharding import PartitionSpec as P

D = 1024
H = 16
DH = 64
PAIR = 2 * DH

NORM_EPS = 1e-05
LEARN_RATE = 0.1
VMEM_LIMIT = 56 * 1024 * 1024
BF = jnp.bfloat16
F32 = jnp.float32


def dot_nn(a, b):
    return lax.dot_general(a, b, (((1,), (0,)), ((), ())), preferred_element_type=F32)


def dot_nt(a, b):
    return lax.dot_general(a, b, (((1,), (1,)), ((), ())), preferred_element_type=F32)


def history_start(lengths_ref, users, place):
    start = jnp.zeros_like(place)
    end = jnp.int32(0)
    for user in range(users - 1):
        end = end + lengths_ref[0, user]
        start = jnp.where(place >= end, end, start)
    return start


def head_columns(kind, head):
    first = head // 2 * 4 * PAIR + head % 2 * 3 * DH + kind * DH
    return slice(first, first + DH)


def gate_columns(pair):
    return slice(pair * 4 * PAIR + 3 * PAIR, (pair + 1) * 4 * PAIR)


def split_pairs(acts_ref, split_ref, kind, block, blk):
    at = pl.ds(pl.multiple_of(block * blk, blk), blk)
    zero = jnp.zeros((blk, DH), BF)
    for p in range(split_ref.shape[0]):
        one, two = (acts_ref[at, head_columns(kind, 2 * p + h)] for h in range(2))
        below = pl.multiple_of(block * 2 * blk + blk, blk)
        split_ref[p, pl.ds(pl.multiple_of(block * 2 * blk, blk), blk), :] = jnp.concatenate([one, zero], axis=1)
        split_ref[p, pl.ds(below, blk), :] = jnp.concatenate([zero, two], axis=1)


def forward_kernel(*refs, blk, users, maxlen, count):
    lengths_ref, order_ref = refs[:2]
    x_refs = refs[2 : 2 + count]
    w_ref = refs[2 + count]
    outs = refs[3 + count :]
    if count > 1:
        x_out_ref, outs = outs[0], outs[1:]
    acts_ref, slopes_ref, gate_ref, weights_ref, score_slope_ref, heads_ref, k_t, v_split = outs
    i = pl.program_id(0)
    heads = weights_ref.shape[0]
    chunks = x_refs[0].shape[0] // blk

    @pl.when(i == 0)
    def _():
        for b in range(count):
            for r in range(chunks):
                at = pl.ds(pl.multiple_of(order_ref[b * chunks + r] * blk, blk), blk)
                x = x_refs[b][r * blk : (r + 1) * blk, :]
                if count > 1:
                    x_out_ref[at, :] = x
                for p in range(heads // 2):
                    lanes = slice(p * 4 * PAIR, (p + 1) * 4 * PAIR)
                    half = 0.5 * dot_nn(x, w_ref[:, lanes])
                    t = jnp.tanh(half)
                    prod = half * t
                    silu = half + prod
                    acts_ref[at, lanes] = silu.astype(BF)
                    gate_ref[at, p * PAIR : (p + 1) * PAIR] = silu[:, 3 * PAIR :]
                    slopes_ref[at, lanes] = (0.5 * (1.0 + t) * (1.0 + half - prod)).astype(BF)
                for h in range(heads):
                    k_t[h * DH : (h + 1) * DH, at] = jnp.transpose(acts_ref[at, head_columns(2, h)])
                split_pairs(acts_ref, v_split, 0, order_ref[b * chunks + r], blk)

    at_i = pl.ds(pl.multiple_of(i * blk, blk), blk)
    q_half = [acts_ref[at_i, head_columns(1, h)] * jnp.asarray(0.5 * DH**-0.5, BF) for h in range(heads)]
    row = i * blk + lax.broadcasted_iota(jnp.int32, (blk, blk), 0)
    col0 = lax.broadcasted_iota(jnp.int32, (blk, blk), 1)
    start = history_start(lengths_ref, users, row)

    def column(j, acc):
        at_j = pl.ds(pl.multiple_of(j * blk, blk), blk)
        both_j = pl.ds(pl.multiple_of(j * 2 * blk, 2 * blk), 2 * blk)
        col = col0 + j * blk
        allowed = (col <= row) & (col >= start)
        per_head = []
        for h in range(heads):
            half = dot_nn(q_half[h], k_t[h * DH : (h + 1) * DH, at_j])
            half = jnp.where(allowed, half, -64.0)
            t = jnp.tanh(half)
            p = half * t
            weights = (half + p).astype(BF)
            weights_ref[h, :, at_j] = weights
            score_slope_ref[h, :, at_j] = ((1.0 + t) * (1.0 + half - p)).astype(BF)
            per_head.append(weights)
        return tuple(
            acc[p] + dot_nn(jnp.concatenate(per_head[2 * p : 2 * p + 2], axis=1), v_split[p, both_j, :])
            for p in range(heads // 2)
        )

    first = history_start(lengths_ref, users, i * blk) // blk
    zero = jnp.zeros((blk, PAIR), F32)
    acc = lax.fori_loop(first, i + 1, column, (zero,) * (heads // 2))
    heads_ref[...] = (jnp.concatenate(acc, axis=1) * (1.0 / maxlen)).astype(BF)


def forward_attention(lengths, order, x_blocks, w_own, blk, maxlen):
    count = len(x_blocks)
    block_rows = x_blocks[0].shape[0]
    positions = count * block_rows
    cols = w_own.shape[1] // 4
    heads = cols // DH
    users = lengths.shape[1]
    elements = heads * positions * positions // 2
    whole = lambda i: (0, 0)
    out_specs = [
        pl.BlockSpec((positions, 4 * cols), whole),
        pl.BlockSpec((positions, 4 * cols), whole),
        pl.BlockSpec((positions, cols), whole),
        pl.BlockSpec((heads, blk, positions), lambda i: (0, i, 0)),
        pl.BlockSpec((heads, blk, positions), lambda i: (0, i, 0)),
        pl.BlockSpec((blk, cols), lambda i: (i, 0)),
    ]
    out_shape = [
        jax.ShapeDtypeStruct((positions, 4 * cols), BF),
        jax.ShapeDtypeStruct((positions, 4 * cols), BF),
        jax.ShapeDtypeStruct((positions, cols), F32),
        jax.ShapeDtypeStruct((heads, positions, positions), BF),
        jax.ShapeDtypeStruct((heads, positions, positions), BF),
        jax.ShapeDtypeStruct((positions, cols), BF),
    ]
    if count > 1:
        out_specs = [pl.BlockSpec((positions, D), whole)] + out_specs
        out_shape = [jax.ShapeDtypeStruct((positions, D), BF)] + out_shape
    return pl.pallas_call(
        functools.partial(forward_kernel, blk=blk, users=users, maxlen=maxlen, count=count),
        grid=(positions // blk,),
        in_specs=[pl.BlockSpec(memory_space=pltpu.SMEM), pl.BlockSpec(memory_space=pltpu.SMEM)]
        + [pl.BlockSpec((block_rows, D), whole)] * count
        + [pl.BlockSpec((D, 4 * cols), whole)],
        out_specs=out_specs,
        out_shape=out_shape,
        scratch_shapes=[pltpu.VMEM((cols, positions), BF), pltpu.VMEM((cols // PAIR, 2 * positions, PAIR), BF)],
        compiler_params=pltpu.CompilerParams(vmem_limit_bytes=VMEM_LIMIT),
        cost_estimate=pl.CostEstimate(
            flops=8 * positions * D * cols + 4 * elements * 256,
            bytes_accessed=4 * positions * D + 4 * elements,
            transcendentals=elements,
        ),
        name="attention_forward",
    )(lengths, order, *x_blocks, w_own)


def stats_kernel(*refs, blk, count):
    order_ref = refs[0]
    og_refs = refs[1 : 1 + count]
    w_ref, gate_ref, heads_ref = refs[1 + count : 4 + count]
    outs = refs[4 + count :]
    if count > 1:
        og_out_ref, outs = outs[0], outs[1:]
    mg_ref, stats_ref = outs
    chunks = og_refs[0].shape[0] // blk
    for b in range(count):
        for r in range(chunks):
            at = pl.ds(pl.multiple_of(order_ref[b * chunks + r] * blk, blk), blk)
            og = og_refs[b][r * blk : (r + 1) * blk, :]
            if count > 1:
                og_out_ref[at, :] = og
            mg = dot_nt(og, w_ref[...])
            mg_ref[at, :] = mg
            ng = mg * gate_ref[at, :]
            heads = heads_ref[at, :].astype(F32)
            mean = jnp.mean(heads, axis=1, keepdims=True)
            centred = heads - mean
            square = jnp.sum(centred * centred, axis=1, keepdims=True)
            total = jnp.sum(ng, axis=1, keepdims=True)
            cross = jnp.sum(ng * centred, axis=1, keepdims=True)
            lane = lax.broadcasted_iota(jnp.int32, (blk, 128), 1)
            packed = jnp.where(lane == 0, mean, jnp.where(lane == 1, square, jnp.where(lane == 2, total, cross)))
            stats_ref[:, at] = jnp.transpose(packed)[:8, :]


def event_stats(order, og_blocks, w_out_own, gate, heads, blk):
    positions, cols = heads.shape
    count = len(og_blocks)
    vmem = pl.BlockSpec(memory_space=pltpu.VMEM)
    out_shape = [
        jax.ShapeDtypeStruct((positions, cols), F32),
        jax.ShapeDtypeStruct((8, positions), F32),
    ]
    if count > 1:
        out_shape = [jax.ShapeDtypeStruct((positions, D), BF)] + out_shape
    return pl.pallas_call(
        functools.partial(stats_kernel, blk=blk, count=count),
        in_specs=[pl.BlockSpec(memory_space=pltpu.SMEM)] + [vmem] * (count + 3),
        out_specs=[vmem] * len(out_shape),
        out_shape=out_shape,
        compiler_params=pltpu.CompilerParams(vmem_limit_bytes=VMEM_LIMIT),
        cost_estimate=pl.CostEstimate(
            flops=2 * positions * cols * D, bytes_accessed=4 * positions * D + 10 * positions * cols, transcendentals=0
        ),
        name="event_stats",
    )(order, *og_blocks, w_out_own, gate, heads)


def combined_stats(stats_refs, cols):
    shards = len(stats_refs)
    positions = stats_refs[0].shape[1]
    means = [ref[0:1, :] for ref in stats_refs]
    mean = sum(means) * (1.0 / shards)
    square = jnp.zeros_like(mean)
    total = jnp.zeros_like(mean)
    cross = jnp.zeros_like(mean)
    for s, ref in enumerate(stats_refs):
        shift = means[s] - mean
        part = ref[2:3, :]
        square = square + ref[1:2, :] + cols * shift * shift
        total = total + part
        cross = cross + ref[3:4, :] + shift * part
    inv_dev = lax.rsqrt(square * (1.0 / D) + NORM_EPS)
    kind = lax.broadcasted_iota(jnp.int32, (128, positions), 0)
    rest = jnp.where(kind == 2, total * (1.0 / D), cross * inv_dev * (1.0 / D))
    packed = jnp.where(kind == 0, mean, jnp.where(kind == 1, inv_dev, rest))
    per_event = jnp.transpose(packed)
    return [per_event[:, k : k + 1] for k in range(4)]


def backward_kernel(*refs, blk, users, maxlen, shards):
    lengths_ref = refs[0]
    stats_refs = refs[1 : 1 + shards]
    mg_ref, gate_ref, heads_ref, acts_ref, slopes_ref, weights_ref, score_slope_ref = refs[1 + shards : 8 + shards]
    grad_ref, mixed_ref, o_ref, o_t, q_t, v_t, k_split, vg_t, kg_t, qg = refs[8 + shards :]
    i = pl.program_id(0)
    positions, cols = o_ref.shape
    heads = cols // DH
    blocks = positions // blk
    scale = DH ** (-0.5)

    @pl.when(i == 0)
    def _():
        mean, inv_dev, total, cross = combined_stats(stats_refs, cols)
        for p in range(heads // 2):
            lanes = slice(p * PAIR, (p + 1) * PAIR)
            normed = (heads_ref[:, lanes].astype(F32) - mean) * inv_dev
            gate = gate_ref[:, lanes]
            mg = mg_ref[:, lanes]
            mixed_ref[:, lanes] = (normed * gate).astype(BF)
            gate_slope = slopes_ref[:, gate_columns(p)].astype(F32)
            grad_ref[:, gate_columns(p)] = (mg * normed * gate_slope).astype(BF)
            o_ref[:, lanes] = (inv_dev * (mg * gate - total - normed * cross)).astype(BF)
        o_t[...] = jnp.transpose(o_ref[...])
        for scratch, kind in ((v_t, 0), (q_t, 1)):
            scratch[...] = jnp.transpose(jnp.concatenate([acts_ref[:, head_columns(kind, h)] for h in range(heads)], axis=1))
        for block in range(blocks):
            split_pairs(acts_ref, k_split, 2, block, blk)
        vg_t[...] = jnp.zeros_like(vg_t)
        kg_t[...] = jnp.zeros_like(kg_t)

    at_i = pl.ds(pl.multiple_of(i * blk, blk), blk)
    o_i = [o_ref[at_i, h * DH : (h + 1) * DH] for h in range(heads)]

    def column(j, acc):
        at_j = pl.ds(pl.multiple_of(j * blk, blk), blk)
        both_j = pl.ds(pl.multiple_of(j * 2 * blk, 2 * blk), 2 * blk)
        per_head = []
        for h in range(heads):
            lanes = slice(h * DH, (h + 1) * DH)
            weight_grad = dot_nn(o_i[h], v_t[lanes, at_j])
            score_grad = (weight_grad * score_slope_ref[h, :, at_j].astype(F32)).astype(BF)
            vg_t[lanes, at_j] += dot_nn(o_t[lanes, at_i], weights_ref[h, :, at_j])
            kg_t[lanes, at_j] += dot_nn(q_t[lanes, at_i], score_grad)
            per_head.append(score_grad)
        return tuple(
            acc[p] + dot_nn(jnp.concatenate(per_head[2 * p : 2 * p + 2], axis=1), k_split[p, both_j, :])
            for p in range(heads // 2)
        )

    first = history_start(lengths_ref, users, i * blk) // blk
    zero = jnp.zeros((blk, PAIR), F32)
    acc = lax.fori_loop(first, i + 1, column, (zero,) * (heads // 2))
    qg[at_i, :] = jnp.concatenate(acc, axis=1)

    @pl.when(i == blocks - 1)
    def _():
        factor = 0.5 * scale / maxlen
        grads = [jnp.transpose(vg_t[...]) * (1.0 / maxlen), qg[...] * factor, jnp.transpose(kg_t[...]) * factor]
        pieces = [grads[kind][:, h * DH : (h + 1) * DH] for h in range(heads) for kind in range(3)]
        for n in range(3 * heads // 2):
            first_lane = n // 3 * 4 * PAIR + n % 3 * PAIR
            lanes = slice(first_lane, first_lane + PAIR)
            grad = jnp.concatenate(pieces[2 * n : 2 * n + 2], axis=1).astype(BF).astype(F32)
            grad_ref[:, lanes] = (grad * slopes_ref[:, lanes].astype(F32)).astype(BF)


def backward_attention(lengths, stats, mg, gate, head_outs, acts, slopes, weights, score_slope, blk, maxlen):
    positions, cols = mg.shape
    heads = cols // DH
    shards = len(stats)
    users = lengths.shape[1]
    elements = heads * positions * positions // 2
    whole = lambda i: (0, 0)
    return pl.pallas_call(
        functools.partial(backward_kernel, blk=blk, users=users, maxlen=maxlen, shards=shards),
        grid=(positions // blk,),
        in_specs=[pl.BlockSpec(memory_space=pltpu.SMEM)]
        + [pl.BlockSpec((8, positions), whole)] * shards
        + [
            pl.BlockSpec((positions, cols), whole),
            pl.BlockSpec((positions, cols), whole),
            pl.BlockSpec((positions, cols), whole),
            pl.BlockSpec((positions, 4 * cols), whole),
            pl.BlockSpec((positions, 4 * cols), whole),
            pl.BlockSpec((heads, blk, positions), lambda i: (0, i, 0)),
            pl.BlockSpec((heads, blk, positions), lambda i: (0, i, 0)),
        ],
        out_specs=[pl.BlockSpec((positions, 4 * cols), whole), pl.BlockSpec((positions, cols), whole)],
        out_shape=[
            jax.ShapeDtypeStruct((positions, 4 * cols), BF),
            jax.ShapeDtypeStruct((positions, cols), BF),
        ],
        scratch_shapes=[
            pltpu.VMEM((positions, cols), BF),
            pltpu.VMEM((cols, positions), BF),
            pltpu.VMEM((cols, positions), BF),
            pltpu.VMEM((cols, positions), BF),
            pltpu.VMEM((cols // PAIR, 2 * positions, PAIR), BF),
            pltpu.VMEM((cols, positions), F32),
            pltpu.VMEM((cols, positions), F32),
            pltpu.VMEM((positions, cols), F32),
        ],
        compiler_params=pltpu.CompilerParams(vmem_limit_bytes=VMEM_LIMIT),
        cost_estimate=pl.CostEstimate(
            flops=8 * elements * 256, bytes_accessed=4 * elements + 26 * positions * cols, transcendentals=0
        ),
        name="attention_backward",
    )(lengths, *stats, mg, gate, head_outs, acts, slopes, weights, score_slope)


def update_kernel(rows_ref, table_ref, accum_ref, new_table_ref, new_accum_ref, ids):
    i = pl.program_id(0)
    blk = table_ref.shape[0]
    slots = rows_ref.shape[0]

    @pl.when(i == 0)
    def _():
        numbers = jnp.transpose(rows_ref[:, D:].astype(F32))
        ids[...] = (numbers[0:1, :] * 256.0 + numbers[1:2, :]).astype(jnp.int32)

    row = i * blk + lax.broadcasted_iota(jnp.int32, (blk, slots), 0)
    hits = jnp.where(row == ids[...], 1.0, 0.0).astype(BF)
    grad = dot_nn(hits, rows_ref[:, :D])
    accum = jnp.transpose(jnp.broadcast_to(accum_ref[...], (128, blk)))[:, :1] + jnp.mean(grad * grad, axis=1, keepdims=True)
    new_accum_ref[...] = jnp.transpose(jnp.broadcast_to(accum, (blk, 128)))[:1, :]
    new_table_ref[...] = table_ref[...] - LEARN_RATE * grad * lax.rsqrt(accum)


def update_rows(got_rows, emb_table, row_accum):
    rows_own = emb_table.shape[0]
    slots = got_rows.shape[0]
    blk = min(256, rows_own)
    new_table, new_accum = pl.pallas_call(
        update_kernel,
        grid=(rows_own // blk,),
        in_specs=[
            pl.BlockSpec((slots, D + 128), lambda i: (0, 0)),
            pl.BlockSpec((blk, D), lambda i: (i, 0)),
            pl.BlockSpec((1, blk), lambda i: (0, i)),
        ],
        out_specs=[
            pl.BlockSpec((blk, D), lambda i: (i, 0)),
            pl.BlockSpec((1, blk), lambda i: (0, i)),
        ],
        out_shape=[
            jax.ShapeDtypeStruct((rows_own, D), F32),
            jax.ShapeDtypeStruct((1, rows_own), F32),
        ],
        scratch_shapes=[pltpu.VMEM((1, slots), jnp.int32)],
        compiler_params=pltpu.CompilerParams(vmem_limit_bytes=VMEM_LIMIT),
        cost_estimate=pl.CostEstimate(
            flops=2 * rows_own * slots * D, bytes_accessed=8 * rows_own * D + 2 * slots * D, transcendentals=rows_own
        ),
        name="update_rows",
    )(got_rows, emb_table, row_accum.reshape(1, rows_own))
    return new_table, new_accum.reshape(rows_own)


def own_weights(w_attn, w_gate, part, pairs):
    slices = []
    for p in range(pairs):
        at = part * pairs + p
        slices.append(lax.dynamic_slice_in_dim(w_attn, at * 3 * PAIR, 3 * PAIR, 1))
        slices.append(lax.dynamic_slice_in_dim(w_gate, at * PAIR, PAIR, 1))
    return jnp.concatenate(slices, axis=1)


def attn_and_gate(proj, pairs):
    pieces = [proj[:, p * 4 * PAIR : (p + 1) * 4 * PAIR] for p in range(pairs)]
    attn = jnp.concatenate([piece[:, : 3 * PAIR] for piece in pieces], axis=1)
    return attn, jnp.concatenate([piece[:, 3 * PAIR :] for piece in pieces], axis=1)


def row_slots(owners, rows, devices, capacity):
    events = owners.shape[0]
    owner_hits = (owners[:, None] == jnp.arange(devices, dtype=jnp.int32)[None, :]).astype(BF)
    place = jnp.arange(events, dtype=jnp.int32)
    before = (place[:, None] > place[None, :]).astype(BF)
    earlier = jnp.dot(before, owner_hits, preferred_element_type=F32)
    slots = jnp.sum(earlier * owner_hits.astype(F32), axis=1).astype(jnp.int32)
    flat_slot = owners * capacity + slots
    slot_hits = jnp.arange(devices * capacity, dtype=jnp.int32)[:, None] == flat_slot[None, :]
    lane = jnp.arange(128, dtype=jnp.int32)[None, :]
    numbers = jnp.where(lane == 0, rows[:, None] // 256, jnp.where(lane == 1, rows[:, None] % 256, 0))
    return slot_hits.astype(BF), numbers.astype(BF)


def rows_to_owners(slot_matrix, input_grad, numbers, devices, capacity):
    rows = jnp.concatenate([input_grad.astype(BF), numbers], axis=1)
    rows = jnp.dot(slot_matrix, rows, preferred_element_type=F32).astype(BF)
    got = lax.all_to_all(
        rows.reshape(devices, capacity, D + 128), ("seq", "dp"), split_axis=0, concat_axis=0, tiled=True
    )
    return got.reshape(devices * capacity, D + 128)


TN = (((0,), (0,)), ((), ()))


def dot_tn(a, b):
    return lax.dot_general(a, b, TN, preferred_element_type=F32)


def body_whole(
    layer_input, out_grad, lengths, item_owner, item_row, w_attn, w_gate, w_out, emb_table, row_accum
):
    seq_count = lax.axis_size("seq")
    dp_count = lax.axis_size("dp")
    devices = seq_count * dp_count
    seq_id = lax.axis_index("seq")
    tokens_dev = layer_input.shape[0]
    positions = tokens_dev * seq_count
    maxlen = 2 * positions // 3
    blk = min(256, positions)
    cols = D // seq_count
    pairs = cols // PAIR
    capacity = max(2, 2 * tokens_dev // devices)

    w_own = own_weights(w_attn, w_gate, seq_id, pairs)
    w_out_own = lax.dynamic_slice_in_dim(w_out, seq_id * cols, cols, 0)
    slot_matrix, numbers = row_slots(item_owner[:, 0], item_row, devices, capacity)

    x_full = lax.all_gather(layer_input, "seq", axis=0, tiled=True)
    og_full = lax.all_gather(out_grad, "seq", axis=0, tiled=True)
    order = jnp.arange(positions // blk, dtype=jnp.int32)
    acts, slopes, gate, weights, score_slope, heads = forward_attention(
        lengths, order, [x_full], w_own, blk, maxlen
    )
    mg, stats_own = event_stats(order, [og_full], w_out_own, gate, heads, blk)
    stats = lax.all_gather(stats_own, "seq", axis=0, tiled=False)
    grads, mixed = backward_attention(
        lengths, [stats[s] for s in range(seq_count)], mg, gate, heads, acts, slopes, weights, score_slope, blk, maxlen
    )

    input_part = dot_nt(grads, w_own).astype(BF)
    got = lax.all_to_all(
        input_part.reshape(seq_count, tokens_dev, D), "seq", split_axis=0, concat_axis=0, tiled=True
    )
    input_grad = jnp.sum(got.astype(F32), axis=0) + out_grad.astype(F32)
    got_rows = rows_to_owners(slot_matrix, input_grad, numbers, devices, capacity)
    new_table, new_accum = update_rows(got_rows, emb_table, row_accum)

    out_part = dot_tn(mixed, og_full).astype(BF)
    share = dp_count // seq_count
    out_part = out_part.reshape(share, D // dp_count, seq_count, cols).transpose(0, 2, 1, 3).reshape(D, cols)
    merged = jnp.concatenate([dot_tn(x_full, grads).astype(BF), out_part], axis=1)
    merged = lax.psum_scatter(merged, "dp", scatter_dimension=0, tiled=True)
    steps = []
    for s in range(seq_count):
        for piece in range(dp_count):
            part, target = divmod(piece, seq_count)
            steps.append((s * dp_count + piece, target * dp_count + s * share + part))
    grad_out = lax.ppermute(merged[:, 4 * cols :], ("seq", "dp"), steps).astype(F32)
    grad_attn, grad_gate = attn_and_gate(merged[:, : 4 * cols].astype(F32), pairs)
    return (grad_attn, grad_gate, grad_out, new_table, new_accum)


SEQ = 4
PLANE = 4


def send(array, target):
    steps = []
    for s in range(SEQ):
        for e in range(PLANE):
            for c in range(2):
                to = target(s, e, c)
                if to is not None:
                    steps.append((s * 2 * PLANE + 2 * e + c, to[0] * 2 * PLANE + 2 * to[1] + to[2]))
    return lax.ppermute(array, ("seq", "dp"), steps)


def home(s, c):
    return c == s // 2


def swap_far(array):
    return send(array, lambda s, e, c: None if home(s, c) else (3 - s, e, 1 - c))


def fetch_near(array):
    return send(array, lambda s, e, c: (s ^ 1, e, c) if home(s, c) else ((3 - s) ^ 1, e, 1 - c))


def swap_near(array):
    return send(array, lambda s, e, c: (s ^ 1, e, c))


def swap_core(array):
    return send(array, lambda s, e, c: (s, e, 1 - c))


def swap_x(array):
    return send(array, lambda s, e, c: (s, e ^ 1, c))


def swap_y(array):
    return send(array, lambda s, e, c: (s, e ^ 2, c))


def tie(*arrays):
    return lax.optimization_barrier(arrays)


def halves(array, bit, axis):
    kept = lax.dynamic_index_in_dim(array, bit, axis, keepdims=False)
    sent = lax.dynamic_index_in_dim(array, 1 - bit, axis, keepdims=False)
    return kept, sent


def body_pairs(
    layer_input, out_grad, lengths, item_owner, item_row, w_attn, w_gate, w_out, emb_table, row_accum
):
    devices = 2 * PLANE * SEQ
    s = lax.axis_index("seq")
    d = lax.axis_index("dp")
    e, c = d // 2, d % 2
    y, x = e // 2, e % 2
    tokens_dev = layer_input.shape[0]
    positions = tokens_dev * SEQ
    maxlen = 2 * positions // 3
    blk = min(256, positions)
    cols = D // SEQ
    pairs = cols // PAIR
    rows_own = emb_table.shape[0]
    capacity = max(2, 2 * tokens_dev // devices)
    at_home = c == s // 2
    part = 2 * (s % 2) + c

    def block_of(seq, core):
        return jnp.where(core == seq // 2, seq, 3 - seq)

    mine_at, near_at = block_of(s, c), block_of(s ^ 1, c)
    core_at, diag_at = block_of(s, 1 - c), block_of(s ^ 1, 1 - c)
    order = jnp.stack([mine_at, near_at, core_at, diag_at]).astype(jnp.int32)

    x_far = swap_far(layer_input)
    x_near = fetch_near(layer_input)
    users = lengths.shape[1]
    keys = (item_owner[:, 0] * rows_own + item_row).reshape(1, tokens_dev)
    small = jnp.concatenate([keys, jnp.pad(lengths, ((0, 0), (0, 128 - users)))], axis=1)
    small = jnp.where(at_home, small, swap_far(small))
    keys, lengths = small[0, :tokens_dev], small[:, tokens_dev : tokens_dev + users]
    w_own = own_weights(w_attn, w_gate, part, pairs)
    w_out_own = lax.dynamic_slice_in_dim(w_out, part * cols, cols, 0)
    slot_matrix, numbers = row_slots(keys // rows_own, keys % rows_own, devices, capacity)
    x_far, x_near, w_own, w_out_own, slot_matrix, numbers, lengths = tie(
        x_far, x_near, w_own, w_out_own, slot_matrix, numbers, lengths
    )
    x_here = jnp.concatenate([jnp.where(at_home, layer_input, x_far), x_near], axis=0)
    x_there = swap_core(x_here)
    x_here, og_own = tie(x_here, out_grad)
    og_far = swap_far(og_own)
    og_near = fetch_near(og_own)

    x_full, acts, slopes, gate, weights, score_slope, heads = forward_attention(
        lengths, order, [x_here, x_there], w_own, blk, maxlen
    )
    og_far, og_near, heads = tie(og_far, og_near, heads)
    og_mine = jnp.where(at_home, og_own, og_far)
    og_here = jnp.concatenate([og_mine, og_near], axis=0)
    og_there = swap_core(og_here)
    og_full, mg, stats_own = event_stats(order, [og_here, og_there], w_out_own, gate, heads, blk)
    stats = [
        stats_own,
        swap_core(stats_own),
        swap_near(stats_own),
        send(stats_own, lambda s, e, c: (s ^ 1, e, 1 - c)),
    ]
    grads, mixed = backward_attention(
        lengths, stats, mg, gate, heads, acts, slopes, weights, score_slope, blk, maxlen
    )

    def input_part(grads, block):
        return dot_nt(lax.dynamic_slice_in_dim(grads, block * tokens_dev, tokens_dev, 0), w_own)

    from_diag = swap_core(input_part(grads, diag_at).astype(BF))
    near_sum = (input_part(grads, near_at) + from_diag.astype(F32)).astype(BF)
    near_sum, grads = tie(near_sum, grads)
    from_near = swap_near(near_sum)
    core_part = input_part(grads, core_at).astype(BF)
    from_core = swap_core(core_part)
    input_grad = input_part(grads, mine_at) + og_mine.astype(F32)

    core_part, grads, mixed = tie(core_part, grads, mixed)
    half = 5 * cols // 2
    proj = dot_tn(x_full, grads).astype(BF).reshape(2, 2, D // PLANE, 4 * cols)
    out_part = dot_tn(mixed, og_full).astype(BF).reshape(cols, 2, 2, cols)
    a_kept, a_sent = halves(proj[..., :half], x, 1)
    b_kept, b_sent = halves(proj[..., half:], y, 0)
    out_kept, out_sent = (piece.transpose(1, 0, 2) for piece in halves(out_part, y, 1))
    b_kept = jnp.concatenate([b_kept, out_kept], axis=-1)
    b_sent = jnp.concatenate([b_sent, out_sent], axis=-1)
    a_got = swap_x(a_sent)
    b_got = swap_y(b_sent)

    input_grad = input_grad + from_core.astype(F32) + from_near.astype(F32)
    got_rows = rows_to_owners(slot_matrix, input_grad, numbers, devices, capacity)

    a = (a_kept.astype(F32) + a_got.astype(F32)).astype(BF)
    b = (b_kept.astype(F32) + b_got.astype(F32)).astype(BF)
    a_kept, a_sent = halves(a, y, 0)
    b_kept, b_sent = halves(b, x, 0)
    a = (a_kept.astype(F32) + swap_y(a_sent).astype(F32)).astype(BF)
    b = (b_kept.astype(F32) + swap_x(b_sent).astype(F32)).astype(BF)

    def last(array, target):
        pieces = array.reshape(2, D // (2 * PLANE), array.shape[1])
        one, other = halves(pieces, s // 2, 0)
        one = send(one, lambda s, e, c: target(s, e, c, s // 2)).astype(F32)
        return one + send(other, lambda s, e, c: target(s, e, c, 1 - s // 2)).astype(F32)

    proj = jnp.concatenate([a, b[:, : 4 * cols - half]], axis=1)
    proj = last(proj, lambda s, e, c, piece: (2 * (s % 2) + c, e, piece))
    grad_out = last(b[:, 4 * cols - half :], lambda s, e, c, piece: (e, 2 * (s % 2) + c, piece))
    grad_attn, grad_gate = attn_and_gate(proj, pairs)
    new_table, new_accum = update_rows(got_rows, emb_table, row_accum)
    return (grad_attn, grad_gate, grad_out, new_table, new_accum)


def solution(mesh):
    placed = (
        P(("dp", "seq"), None),
        P(("dp", "seq"), None),
        P("dp", None),
        P(("dp", "seq"), None),
        P(("dp", "seq")),
        P(),
        P(),
        P(),
        P(("seq", "dp"), None),
        P(("seq", "dp")),
    )
    paired = mesh.shape["seq"] == SEQ and mesh.shape["dp"] == 2 * PLANE
    return jax.shard_map(
        body_pairs if paired else body_whole,
        mesh=mesh,
        in_specs=placed,
        out_specs=(
            P("dp", "seq"),
            P("dp", "seq"),
            P("dp", "seq"),
            P(("seq", "dp"), None),
            P(("seq", "dp")),
        ),
        check_vma=False,
    )
```

profile of v0, /device:TPU:0, one launch (start us, length us, event | category | flops | bytes accessed | tf_op | source)
XLA Modules:
  0.0 172.6 jit_solution(12329071526577994868)
XLA Ops:
  1.5 3.1 %collective-permute-start.1 = (bf16[256,1024]{1,0:T(8,128)(2,1)}, bf16[256,1024]{1,0:T(8,128)(2,1)S(1)}, u32[]{:S(2)}, u32[]{:S(2)}) collective-permute-start(bf16[256,1024]{1,0:T(8,128)(2,1)} %param.10), channel_id=1, source_target_pairs={{0,8},{1,16},{2,10},{3,18},{4,12},{5,20},{6,14},{7,22},{8,0},{9,24... | collective-permute-start | bytes 1572872 | tf_op jit(solution)/shard_map/ppermute | solution.py:514
  9.2 1.5 constant_dynamic-slice_fusion.6
  10.8 1.6 pad_maximum_fusion.refs_4_
  14.7 16.3 %collective-permute-start.3 = (bf16[512,1024]{1,0:T(8,128)(2,1)S(1)}, bf16[512,1024]{1,0:T(8,128)(2,1)}, u32[]{:S(2)}, u32[]{:S(2)}) collective-permute-start(bf16[512,1024]{1,0:T(8,128)(2,1)S(1)} %pad_maximum_fusion.1.refs_2_), channel_id=1, source_target_pairs={{0,1},{1,0},{2,3},{3,2},{4,5},{5,4},{6,7},{7,6},{8,9},{9,8},{10,11... | collective-permute-start | bytes 3145736 | tf_op jit(solution)/shard_map/ppermute | solution.py:514
  31.7 1.7 collective-permute-start.5
  34.0 16.8 %attention_forward.1 = (bf16[1024,1024]{1,0:T(8,128)(2,1)}, bf16[1024,1024]{1,0:T(8,128)(2,1)}, bf16[1024,1024]{1,0:T(8,128)(2,1)}, f32[1024,256]{1,0:T(8,128)},...) custom-call(s32[1,3]{1,0:T(1,128)} %slice.47.refs_0_, ...), custom_call_target="tpu_custom_call" | custom-call | flops 4294967296 | bytes 12582912 | tf_op jit(solution)/shard_map/attention_forward/pallas_call | solution.py:151
  51.0 8.7 %collective-permute-start.6 = (bf16[512,1024]{1,0:T(8,128)(2,1)S(1)}, bf16[512,1024]{1,0:T(8,128)(2,1)S(1)}, u32[]{:S(2)}, u32[]{:S(2)}) collective-permute-start(bf16[512,1024]{1,0:T(8,128)(2,1)S(1)} %pad_maximum_fusion.2.refs_1_), channel_id=1, source_target_pairs={{0,1},{1,0},{2,3},{3,2},{4,5},{5,4},{6,7},{7,6},{8,9},{9,8},{10,11... | collective-permute-start | bytes 3145736 | tf_op jit(solution)/shard_map/ppermute | solution.py:514
  59.7 2.3 %collective-permute-done.6.refs_2_ = bf16[512,1024]{1,0:T(8,128)(2,1)S(1)} collective-permute-done((bf16[512,1024]{1,0:T(8,128)(2,1)S(1)}, bf16[512,1024]{1,0:T(8,128)(2,1)S(1)}, u32[]{:S(2)}, u32[]{:S(2)}) %collective-permute-start.6) | collective-permute-done | bytes 1048608 | tf_op jit(solution)/shard_map/ppermute | solution.py:514
  62.9 4.6 %event_stats.1 = (bf16[1024,1024]{1,0:T(8,128)(2,1)}, f32[1024,256]{1,0:T(8,128)}, f32[8,1024]{1,0:T(8,128)}) custom-call(s32[4]{0:T(128)} %pad_add_fusion.1.refs_1_.refs_0_, bf16[512,1024]{1,0:T(8,128)(2,1)} %copy-done.3, bf16[512,1024]{1,0:T(8,128)(2,1)} %copy-done.8, bf16[256,1024]{1,0:T(8,128)(2,1)} %constant_dynamic-slice_fusion.2.refs_3_, ...), custom_call_target="tpu_custom_call" | custom-call | flops 536870912 | bytes 6815744 | tf_op jit(solution)/shard_map/event_stats/pallas_call | solution.py:209
  67.9 1.5 collective-permute-start.9
  69.4 2.6 %collective-permute-done.8.refs_3_ = f32[8,1024]{1,0:T(8,128)S(1)} collective-permute-done((f32[8,1024]{1,0:T(8,128)}, f32[8,1024]{1,0:T(8,128)S(1)}, u32[]{:S(2)}, u32[]{:S(2)}) %collective-permute-start.8) | collective-permute-done | bytes 32800 | tf_op jit(solution)/shard_map/ppermute | solution.py:514
  72.6 15.9 %attention_backward.1 = (bf16[1024,1024]{1,0:T(8,128)(2,1)}, bf16[1024,256]{1,0:T(8,128)(2,1)}) custom-call(s32[1,3]{1,0:T(1,128)} %slice.47.refs_0_, f32[8,1024]{1,0:T(8,128)} %get-tuple-element.48.refs_1_, f32[8,1024]{1,0:T(8,128)} %copy-done.13, f32[8,1024]{1,0:T(8,128)} %copy-done.14, f32[8,1024]{1,0:T(8,128)} %copy-done.15, ...), custom_call_target="tpu_custom_call" | custom-call | flops 4294967296 | bytes 15204352 | tf_op jit(solution)/shard_map/attention_backward/pallas_call | solution.py:318
  88.6 1.8 %convolution_convert_fusion.4 = bf16[256,1024]{1,0:T(8,128)(2,1)S(1)} fusion(bf16[1024,1024]{1,0:T(8,128)(2,1)S(1)} %copy-done.5, bf16[1024,1024]{1,0:T(8,128)(2,1)} %get-tuple-element.57, s32[]{:T(128)S(6)} %select_n.201), kind=kOutput, calls=%fused_computation.12 | convolution fusion | flops 537133056 | bytes 3145732 | tf_op jit(solution)/shard_map/dot_general | solution.py:27
  90.6 1.9 %collective-permute-done.10 = bf16[256,1024]{1,0:T(8,128)(2,1)} collective-permute-done((bf16[256,1024]{1,0:T(8,128)(2,1)S(1)}, bf16[256,1024]{1,0:T(8,128)(2,1)}, u32[]{:S(2)}, u32[]{:S(2)}) %collective-permute-start.10) | collective-permute-done | bytes 524320 | tf_op jit(solution)/shard_map/ppermute | solution.py:514
  92.5 2.7 %fusion.3 = bf16[256,1024]{1,0:T(8,128)(2,1)} fusion(bf16[1024,1024]{1,0:T(8,128)(2,1)S(1)} %copy-done.5, bf16[256,1024]{1,0:T(8,128)(2,1)} %collective-permute-done.10, bf16[1024,1024]{1,0:T(8,128)(2,1)} %get-tuple-element.57, s32[]{:T(128)S(6)} %select_n.200), kind=kOutput, calls=%fused_computation.13 | convolution fusion | flops 537657344 | bytes 3670020 | tf_op jit(solution)/shard_map/dot_general | solution.py:27
  95.2 1.6 convolution_convert_fusion.3
  97.0 1.7 %collective-permute-start.20 = (bf16[256,1024]{1,0:T(8,128)(2,1)}, bf16[256,1024]{1,0:T(8,128)(2,1)}, u32[]{:S(2)}, u32[]{:S(2)}) collective-permute-start(bf16[256,1024]{1,0:T(8,128)(2,1)} %fusion.3), channel_id=1, source_target_pairs={{0,8},{1,9},{2,10},{3,11},{4,12},{5,13},{6,14},{7,15},{8,0},{9,1},... | collective-permute-start | bytes 1572872 | tf_op jit(solution)/shard_map/ppermute | solution.py:514
  98.7 2.4 %convolution_convert_fusion.1 = bf16[1024,1024]{1,0:T(8,128)(2,1)S(1)} fusion(bf16[1024,1024]{1,0:T(8,128)(2,1)S(1)} %copy-done.18, bf16[1024,1024]{1,0:T(8,128)(2,1)S(1)} %copy-done.17), kind=kOutput, calls=%fused_computation.2 | convolution fusion | flops 2148532224 | bytes 6291456 | tf_op jit(solution)/shard_map/dot_general | solution.py:445
  101.2 1.5 convolution_convert_fusion.2
  102.9 1.4 reshape.171
  106.6 1.7 collective-permute-start.13
  111.5 2.3 %fusion.4 = bf16[256,1024]{1,0:T(8,128)(2,1)S(1)} fusion(bf16[1024,1024]{1,0:T(8,128)(2,1)S(1)} %copy-done.6, bf16[256,1024]{1,0:T(8,128)(2,1)} %collective-permute-done.20, bf16[256,1024]{1,0:T(8,128)(2,1)} %collective-permute-done.19, bf16[256,1024]{1,0:T(8,128)(2,1)S(1)} %broadcast_select_fusion, bf16[1024,1024]{1,0:T(8,128)(2,1)} %get-tuple-element.57, ...), kind=kOutput, calls=%fused_computation.14 | convolution fusion | flops 538705920 | bytes 4718596 | tf_op jit(solution)/shard_map/dot_general | solution.py:27
  113.8 1.5 convolution_convert_fusion
  115.3 5.5 %all-to-all-start = ((bf16[32,16,1152]{2,1,0:T(8,128)(2,1)}), bf16[32,16,1152]{2,1,0:T(8,128)(2,1)S(1)}, u32[]{:S(2)}, u32[]{:S(2)}) async-start(bf16[32,16,1152]{2,1,0:T(8,128)(2,1)} %bitcast.28), calls=%async_computation | async-start | bytes 2359296 | tf_op jit(solution)/shard_map/all_to_all | solution.py:435
  120.8 2.8 %collective-permute-done.13 = bf16[2,256,640]{2,1,0:T(8,128)(2,1)} collective-permute-done((bf16[2,256,640]{2,1,0:T(8,128)(2,1)}, bf16[2,256,640]{2,1,0:T(8,128)(2,1)}, u32[]{:S(2)}, u32[]{:S(2)}) %collective-permute-start.13) | collective-permute-done | bytes 655392 | tf_op jit(solution)/shard_map/ppermute | solution.py:514
  124.9 3.8 %collective-permute-start.14 = (bf16[256,640]{1,0:T(8,128)(2,1)S(1)}, bf16[256,640]{1,0:T(8,128)(2,1)S(1)}, u32[]{:S(2)}, u32[]{:S(2)}) collective-permute-start(bf16[256,640]{1,0:T(8,128)(2,1)S(1)} %dynamic-slice_bitcast_fusion.3), channel_id=1, source_target_pairs={{0,2},{1,3},{2,0},{3,1},{4,6},{5,7},{6,4},{7,5},{8,10},{9,11},{10,... | collective-permute-start | bytes 983048 | tf_op jit(solution)/shard_map/ppermute | solution.py:514
  128.6 1.5 collective-permute-done.11
  132.7 11.3 %collective-permute-done.14 = bf16[256,640]{1,0:T(8,128)(2,1)S(1)} collective-permute-done((bf16[256,640]{1,0:T(8,128)(2,1)S(1)}, bf16[256,640]{1,0:T(8,128)(2,1)S(1)}, u32[]{:S(2)}, u32[]{:S(2)}) %collective-permute-start.14) | collective-permute-done | bytes 327712 | tf_op jit(solution)/shard_map/ppermute | solution.py:514
  144.8 2.8 %collective-permute-start.18 = (bf16[128,256]{1,0:T(8,128)(2,1)S(1)}, bf16[128,256]{1,0:T(8,128)(2,1)S(1)}, u32[]{:S(2)}, u32[]{:S(2)}) collective-permute-start(bf16[128,256]{1,0:T(8,128)(2,1)S(1)} %get-tuple-element.82), channel_id=1, source_target_pairs={{0,1},{1,3},{2,9},{3,11},{4,17},{5,19},{6,25},{7,27},{8,5},{9,7},{... | collective-permute-start | bytes 196616 | tf_op jit(solution)/shard_map/ppermute | solution.py:514
  148.5 6.3 %collective-permute-start.16 = (bf16[128,1024]{1,0:T(8,128)(2,1)S(1)}, bf16[128,1024]{1,0:T(8,128)(2,1)S(1)}, u32[]{:S(2)}, u32[]{:S(2)}) collective-permute-start(bf16[128,1024]{1,0:T(8,128)(2,1)S(1)} %get-tuple-element.78), channel_id=1, source_target_pairs={{0,1},{1,9},{2,3},{3,11},{4,5},{5,13},{6,7},{7,15},{8,17},{9,25},{... | collective-permute-start | bytes 786440 | tf_op jit(solution)/shard_map/ppermute | solution.py:514
  155.5 10.3 %collective-permute-done.16 = bf16[128,1024]{1,0:T(8,128)(2,1)S(1)} collective-permute-done((bf16[128,1024]{1,0:T(8,128)(2,1)S(1)}, bf16[128,1024]{1,0:T(8,128)(2,1)S(1)}, u32[]{:S(2)}, u32[]{:S(2)}) %collective-permute-start.16) | collective-permute-done | bytes 262176 | tf_op jit(solution)/shard_map/ppermute | solution.py:514
  168.4 4.2 %update_rows.1 = (f32[512,1024]{1,0:T(8,128)}, f32[1,512]{1,0:T(1,128)}) custom-call(bf16[512,1152]{1,0:T(8,128)(2,1)} %bitcast.62, f32[512,1024]{1,0:T(8,128)} %table_ref.1, f32[1,512]{1,0:T(1,128)} %bitcast.75), custom_call_target="tpu_custom_call" | custom-call | flops 536870912 | bytes 5242880 | tf_op jit(solution)/shard_map/update_rows/pallas_call | solution.py:377
  (110 shorter events, 25.9 us)
Async XLA Ops:
  0.6 6.7 %copy-start = (bf16[1024,1024]{1,0:T(8,128)(2,1)S(1)}, bf16[1024,1024]{1,0:T(8,128)(2,1)}, u32[]{:S(2)}) copy-start(bf16[1024,1024]{1,0:T(8,128)(2,1)} %param.17) | copy-start | bytes 6291460
  0.6 12.8 %collective-permute-start = (bf16[256,1024]{1,0:T(8,128)(2,1)}, bf16[256,1024]{1,0:T(8,128)(2,1)S(1)}, u32[]{:S(2)}, u32[]{:S(2)}) collective-permute-start(bf16[256,1024]{1,0:T(8,128)(2,1)} %param.10), channel_id=1, source_target_pairs={{1,24},{3,26},{5,28},{7,30},{9,16},{11,18},{13,20},{15,22},{16,9},... | collective-permute-start | bytes 1572872 | tf_op jit(solution)/shard_map/ppermute | solution.py:514
  1.5 13.1 %collective-permute-start.1 = (bf16[256,1024]{1,0:T(8,128)(2,1)}, bf16[256,1024]{1,0:T(8,128)(2,1)S(1)}, u32[]{:S(2)}, u32[]{:S(2)}) collective-permute-start(bf16[256,1024]{1,0:T(8,128)(2,1)} %param.10), channel_id=1, source_target_pairs={{0,8},{1,16},{2,10},{3,18},{4,12},{5,20},{6,14},{7,22},{8,0},{9,24... | collective-permute-start | bytes 1572872 | tf_op jit(solution)/shard_map/ppermute | solution.py:514
  6.6 5.8 %collective-permute-start.2 = (s32[1,384]{1,0:T(1,128)S(1)}, s32[1,384]{1,0:T(1,128)S(1)}, u32[]{:S(2)}, u32[]{:S(2)}) collective-permute-start(s32[1,384]{1,0:T(1,128)S(1)} %pad_add_fusion), channel_id=1, source_target_pairs={{1,24},{3,26},{5,28},{7,30},{9,16},{11,18},{13,20},{15,22},{16,9},... | collective-permute-start | bytes 4616 | tf_op jit(solution)/shard_map/ppermute | solution.py:514
  10.8 3.8 %copy-start.10 = (bf16[256,1024]{1,0:T(8,128)(2,1)S(1)}, bf16[256,1024]{1,0:T(8,128)(2,1)}, u32[]{:S(2)}) copy-start(bf16[256,1024]{1,0:T(8,128)(2,1)} %param.10) | copy-start | bytes 1572868
  12.4 18.6 %copy-start.11 = (bf16[256,1024]{1,0:T(8,128)(2,1)S(1)}, bf16[256,1024]{1,0:T(8,128)(2,1)}, u32[]{:S(2)}) copy-start(bf16[256,1024]{1,0:T(8,128)(2,1)} %param.11) | copy-start | bytes 1572868
  14.7 19.3 %copy-start.9 = (bf16[512,1024]{1,0:T(8,128)(2,1)}, bf16[512,1024]{1,0:T(8,128)(2,1)S(1)}, u32[]{:S(2)}) copy-start(bf16[512,1024]{1,0:T(8,128)(2,1)S(1)} %pad_maximum_fusion.1.refs_2_) | copy-start | bytes 3145732
  14.7 19.3 %collective-permute-start.3 = (bf16[512,1024]{1,0:T(8,128)(2,1)S(1)}, bf16[512,1024]{1,0:T(8,128)(2,1)}, u32[]{:S(2)}, u32[]{:S(2)}) collective-permute-start(bf16[512,1024]{1,0:T(8,128)(2,1)S(1)} %pad_maximum_fusion.1.refs_2_), channel_id=1, source_target_pairs={{0,1},{1,0},{2,3},{3,2},{4,5},{5,4},{6,7},{7,6},{8,9},{9,8},{10,11... | collective-permute-start | bytes 3145736 | tf_op jit(solution)/shard_map/ppermute | solution.py:514
  31.0 19.8 %collective-permute-start.4 = (bf16[256,1024]{1,0:T(8,128)(2,1)S(1)}, bf16[256,1024]{1,0:T(8,128)(2,1)S(1)}, u32[]{:S(2)}, u32[]{:S(2)}) collective-permute-start(bf16[256,1024]{1,0:T(8,128)(2,1)S(1)} %copy-done.11), channel_id=1, source_target_pairs={{1,24},{3,26},{5,28},{7,30},{9,16},{11,18},{13,20},{15,22},{16,9},... | collective-permute-start | bytes 1572872 | tf_op jit(solution)/shard_map/ppermute | solution.py:514
  31.7 19.1 %collective-permute-start.5 = (bf16[256,1024]{1,0:T(8,128)(2,1)S(1)}, bf16[256,1024]{1,0:T(8,128)(2,1)S(1)}, u32[]{:S(2)}, u32[]{:S(2)}) collective-permute-start(bf16[256,1024]{1,0:T(8,128)(2,1)S(1)} %copy-done.11), channel_id=1, source_target_pairs={{0,8},{1,16},{2,10},{3,18},{4,12},{5,20},{6,14},{7,22},{8,0},{9,24... | collective-permute-start | bytes 1572872 | tf_op jit(solution)/shard_map/ppermute | solution.py:514
  51.0 11.0 %copy-start.3 = (bf16[512,1024]{1,0:T(8,128)(2,1)}, bf16[512,1024]{1,0:T(8,128)(2,1)S(1)}, u32[]{:S(2)}) copy-start(bf16[512,1024]{1,0:T(8,128)(2,1)S(1)} %pad_maximum_fusion.2.refs_1_) | copy-start | bytes 3145732
  51.0 11.0 %collective-permute-start.6 = (bf16[512,1024]{1,0:T(8,128)(2,1)S(1)}, bf16[512,1024]{1,0:T(8,128)(2,1)S(1)}, u32[]{:S(2)}, u32[]{:S(2)}) collective-permute-start(bf16[512,1024]{1,0:T(8,128)(2,1)S(1)} %pad_maximum_fusion.2.refs_1_), channel_id=1, source_target_pairs={{0,1},{1,0},{2,3},{3,2},{4,5},{5,4},{6,7},{7,6},{8,9},{9,8},{10,11... | collective-permute-start | bytes 3145736 | tf_op jit(solution)/shard_map/ppermute | solution.py:514
  67.5 1.9 %collective-permute-start.7 = (f32[8,1024]{1,0:T(8,128)}, f32[8,1024]{1,0:T(8,128)S(1)}, u32[]{:S(2)}, u32[]{:S(2)}) collective-permute-start(f32[8,1024]{1,0:T(8,128)} %get-tuple-element.48.refs_1_), channel_id=1, source_target_pairs={{0,1},{1,0},{2,3},{3,2},{4,5},{5,4},{6,7},{7,6},{8,9},{9,8},{10,11... | collective-permute-start | bytes 98312 | tf_op jit(solution)/shard_map/ppermute | solution.py:514
  67.9 4.1 %collective-permute-start.8 = (f32[8,1024]{1,0:T(8,128)}, f32[8,1024]{1,0:T(8,128)S(1)}, u32[]{:S(2)}, u32[]{:S(2)}) collective-permute-start(f32[8,1024]{1,0:T(8,128)} %get-tuple-element.48.refs_1_), channel_id=1, source_target_pairs={{0,8},{1,9},{2,10},{3,11},{4,12},{5,13},{6,14},{7,15},{8,0},{9,1},... | collective-permute-start | bytes 98312 | tf_op jit(solution)/shard_map/ppermute | solution.py:514
  67.9 4.1 %collective-permute-start.9 = (f32[8,1024]{1,0:T(8,128)}, f32[8,1024]{1,0:T(8,128)S(1)}, u32[]{:S(2)}, u32[]{:S(2)}) collective-permute-start(f32[8,1024]{1,0:T(8,128)} %get-tuple-element.48.refs_1_), channel_id=1, source_target_pairs={{0,9},{1,8},{2,11},{3,10},{4,13},{5,12},{6,15},{7,14},{8,1},{9,0},... | collective-permute-start | bytes 98312 | tf_op jit(solution)/shard_map/ppermute | solution.py:514
  72.6 15.9 %copy-start.5 = (bf16[1024,1024]{1,0:T(8,128)(2,1)S(1)}, bf16[1024,1024]{1,0:T(8,128)(2,1)}, u32[]{:S(2)}) copy-start(bf16[1024,1024]{1,0:T(8,128)(2,1)} %pad_maximum_fusion.refs_4_) | copy-start | bytes 6291460
  90.4 2.1 %collective-permute-start.10 = (bf16[256,1024]{1,0:T(8,128)(2,1)S(1)}, bf16[256,1024]{1,0:T(8,128)(2,1)}, u32[]{:S(2)}, u32[]{:S(2)}) collective-permute-start(bf16[256,1024]{1,0:T(8,128)(2,1)S(1)} %convolution_convert_fusion.4), channel_id=1, source_target_pairs={{0,1},{1,0},{2,3},{3,2},{4,5},{5,4},{6,7},{7,6},{8,9},{9,8},{10,11... | collective-permute-start | bytes 1572872 | tf_op jit(solution)/shard_map/ppermute | solution.py:514
  90.6 4.6 %copy-start.17 = (bf16[1024,1024]{1,0:T(8,128)(2,1)S(1)}, bf16[1024,1024]{1,0:T(8,128)(2,1)}, u32[]{:S(2)}) copy-start(bf16[1024,1024]{1,0:T(8,128)(2,1)} %get-tuple-element.57) | copy-start | bytes 6291460
  96.8 13.8 %collective-permute-start.19 = (bf16[256,1024]{1,0:T(8,128)(2,1)}, bf16[256,1024]{1,0:T(8,128)(2,1)}, u32[]{:S(2)}, u32[]{:S(2)}) collective-permute-start(bf16[256,1024]{1,0:T(8,128)(2,1)} %convolution_convert_fusion.3), channel_id=1, source_target_pairs={{0,1},{1,0},{2,3},{3,2},{4,5},{5,4},{6,7},{7,6},{8,9},{9,8},{10,11... | collective-permute-start | bytes 1572872 | tf_op jit(solution)/shard_map/ppermute | solution.py:514
  97.0 14.5 %collective-permute-start.20 = (bf16[256,1024]{1,0:T(8,128)(2,1)}, bf16[256,1024]{1,0:T(8,128)(2,1)}, u32[]{:S(2)}, u32[]{:S(2)}) collective-permute-start(bf16[256,1024]{1,0:T(8,128)(2,1)} %fusion.3), channel_id=1, source_target_pairs={{0,8},{1,9},{2,10},{3,11},{4,12},{5,13},{6,14},{7,15},{8,0},{9,1},... | collective-permute-start | bytes 1572872 | tf_op jit(solution)/shard_map/ppermute | solution.py:514
  104.8 6.7 %copy-start.6 = (bf16[1024,1024]{1,0:T(8,128)(2,1)S(1)}, bf16[1024,1024]{1,0:T(8,128)(2,1)}, u32[]{:S(2)}) copy-start(bf16[1024,1024]{1,0:T(8,128)(2,1)} %pad_maximum_fusion.refs_4_) | copy-start | bytes 6291460
  106.6 17.0 %collective-permute-start.13 = (bf16[2,256,640]{2,1,0:T(8,128)(2,1)}, bf16[2,256,640]{2,1,0:T(8,128)(2,1)}, u32[]{:S(2)}, u32[]{:S(2)}) collective-permute-start(bf16[2,256,640]{2,1,0:T(8,128)(2,1)} %pad_maximum_fusion.3), channel_id=1, source_target_pairs={{0,4},{1,5},{2,6},{3,7},{4,0},{5,1},{6,2},{7,3},{8,12},{9,13},{10,... | collective-permute-start | bytes 1966088 | tf_op jit(solution)/shard_map/ppermute | solution.py:514
  109.2 21.0 %collective-permute-start.11 = (bf16[2,256,640]{2,1,0:T(8,128)(2,1)}, bf16[2,256,640]{2,1,0:T(8,128)(2,1)}, u32[]{:S(2)}, u32[]{:S(2)}) collective-permute-start(bf16[2,256,640]{2,1,0:T(8,128)(2,1)} %dynamic-slice_bitcast_fusion), channel_id=1, source_target_pairs={{0,2},{1,3},{2,0},{3,1},{4,6},{5,7},{6,4},{7,5},{8,10},{9,11},{10,... | collective-permute-start | bytes 1966088 | tf_op jit(solution)/shard_map/ppermute | solution.py:514
  113.8 9.8 %copy-start.7 = (bf16[2,256,384]{2,1,0:T(8,128)(2,1)S(1)}, bf16[2,256,384]{2,1,0:T(8,128)(2,1)}, u32[]{:S(2)}) copy-start(bf16[2,256,384]{2,1,0:T(8,128)(2,1)} %get-tuple-element.71) | copy-start | bytes 1179652
  115.3 52.1 %all-to-all-start = ((bf16[32,16,1152]{2,1,0:T(8,128)(2,1)}), bf16[32,16,1152]{2,1,0:T(8,128)(2,1)S(1)}, u32[]{:S(2)}, u32[]{:S(2)}) async-start(bf16[32,16,1152]{2,1,0:T(8,128)(2,1)} %bitcast.28), calls=%async_computation | async-start | bytes 2359296 | tf_op jit(solution)/shard_map/all_to_all | solution.py:435
  124.9 19.1 %collective-permute-start.14 = (bf16[256,640]{1,0:T(8,128)(2,1)S(1)}, bf16[256,640]{1,0:T(8,128)(2,1)S(1)}, u32[]{:S(2)}, u32[]{:S(2)}) collective-permute-start(bf16[256,640]{1,0:T(8,128)(2,1)S(1)} %dynamic-slice_bitcast_fusion.3), channel_id=1, source_target_pairs={{0,2},{1,3},{2,0},{3,1},{4,6},{5,7},{6,4},{7,5},{8,10},{9,11},{10,... | collective-permute-start | bytes 983048 | tf_op jit(solution)/shard_map/ppermute | solution.py:514
  131.5 16.1 %collective-permute-start.12 = (bf16[256,640]{1,0:T(8,128)(2,1)S(1)}, bf16[256,640]{1,0:T(8,128)(2,1)S(1)}, u32[]{:S(2)}, u32[]{:S(2)}) collective-permute-start(bf16[256,640]{1,0:T(8,128)(2,1)S(1)} %dynamic-slice_bitcast_fusion.4), channel_id=1, source_target_pairs={{0,4},{1,5},{2,6},{3,7},{4,0},{5,1},{6,2},{7,3},{8,12},{9,13},{10,... | collective-permute-start | bytes 983048 | tf_op jit(solution)/shard_map/ppermute | solution.py:514
  144.1 10.7 %collective-permute-start.17 = (bf16[128,256]{1,0:T(8,128)(2,1)S(1)}, bf16[128,256]{1,0:T(8,128)(2,1)S(1)}, u32[]{:S(2)}, u32[]{:S(2)}) collective-permute-start(bf16[128,256]{1,0:T(8,128)(2,1)S(1)} %get-tuple-element.81), channel_id=1, source_target_pairs={{0,0},{1,2},{2,8},{3,10},{4,16},{5,18},{6,24},{7,26},{8,4},{9,6},{... | collective-permute-start | bytes 196616 | tf_op jit(solution)/shard_map/ppermute | solution.py:514
  144.8 10.0 %collective-permute-start.18 = (bf16[128,256]{1,0:T(8,128)(2,1)S(1)}, bf16[128,256]{1,0:T(8,128)(2,1)S(1)}, u32[]{:S(2)}, u32[]{:S(2)}) collective-permute-start(bf16[128,256]{1,0:T(8,128)(2,1)S(1)} %get-tuple-element.82), channel_id=1, source_target_pairs={{0,1},{1,3},{2,9},{3,11},{4,17},{5,19},{6,25},{7,27},{8,5},{9,7},{... | collective-permute-start | bytes 196616 | tf_op jit(solution)/shard_map/ppermute | solution.py:514
  147.8 7.7 %collective-permute-start.15 = (bf16[128,1024]{1,0:T(8,128)(2,1)S(1)}, bf16[128,1024]{1,0:T(8,128)(2,1)S(1)}, u32[]{:S(2)}, u32[]{:S(2)}) collective-permute-start(bf16[128,1024]{1,0:T(8,128)(2,1)S(1)} %get-tuple-element.77), channel_id=1, source_target_pairs={{0,0},{1,8},{2,2},{3,10},{4,4},{5,12},{6,6},{7,14},{8,16},{9,24},{... | collective-permute-start | bytes 786440 | tf_op jit(solution)/shard_map/ppermute | solution.py:514
  148.5 17.3 %collective-permute-start.16 = (bf16[128,1024]{1,0:T(8,128)(2,1)S(1)}, bf16[128,1024]{1,0:T(8,128)(2,1)S(1)}, u32[]{:S(2)}, u32[]{:S(2)}) collective-permute-start(bf16[128,1024]{1,0:T(8,128)(2,1)S(1)} %get-tuple-element.78), channel_id=1, source_target_pairs={{0,1},{1,9},{2,3},{3,11},{4,5},{5,13},{6,7},{7,15},{8,17},{9,25},{... | collective-permute-start | bytes 786440 | tf_op jit(solution)/shard_map/ppermute | solution.py:514
  166.6 6.1 %copy-start.1 = (bf16[1024,1024]{1,0:T(8,128)(2,1)S(1)}, bf16[1024,1024]{1,0:T(8,128)(2,1)}, u32[]{:S(2)}) copy-start(bf16[1024,1024]{1,0:T(8,128)(2,1)} %param.17) | copy-start | bytes 6291460
  (9 other events, 16.0 us)
where the time goes:
time: 173 us
  starting transfers between devices  59.9 us (35%)
  Pallas kernels  41.5 us (24%)
  waiting for transfers between devices  34.7 us (20%)
  matrix products  14.1 us (8%)
  local copies, waits for them, and re-layouts  10.8 us (6%)
  other arithmetic  10.6 us (6%)
    ppermute x21, starting transfers between devices, send(): return lax.ppermute(array, ('seq', 'dp'), steps)  54.4 us
    ppermute x21, waiting for transfers between devices, send(): return lax.ppermute(array, ('seq', 'dp'), steps)  34.7 us
    pallas_call x1, Pallas kernels, forward_attention(): pl.pallas_call(functools.partial(forward_kernel, blk=blk, users=users, ma...  16.8 us
    pallas_call x1, Pallas kernels, backward_attention(): pl.pallas_call(functools.partial(backward_kernel, blk=blk, users=users, m...  15.9 us
    dot_general x4, matrix products, dot_nt(): lax.dot_general(a, b, (((1,), (1,)), ((), ())), preferred_element_type=F32)  8.4 us
    all_to_all x1, starting transfers between devices, rows_to_owners(): lax.all_to_all(rows.reshape(devices, capacity, D + 128), ('seq', 'dp'), s...  5.5 us
    pallas_call x1, Pallas kernels, event_stats(): pl.pallas_call(functools.partial(stats_kernel, blk=blk, count=count), in_...  4.6 us
    pallas_call x1, Pallas kernels, update_rows(): pl.pallas_call(update_kernel, grid=(rows_own // blk,), in_specs=[pl.Block...  4.2 us
  transfers between devices with their start and end apart: 22, of which 9 were waited for; matrix products, arithmetic and copies ran while one was open for 15% of the time, Pallas kernels for 10%

commit v1 on v0

--- a/solution.py
+++ b/solution.py
@@ -62,10 +62,20 @@
     outs = refs[3 + count :]
     if count > 1:
         x_out_ref, outs = outs[0], outs[1:]
-    acts_ref, slopes_ref, gate_ref, weights_ref, score_slope_ref, heads_ref, k_t, v_split = outs
+    acts_out, slopes_out, gate_out, weights_ref, score_slope_ref, heads_ref = outs[:6]
+    k_t, v_split, acts_ref, slopes_ref, gate_ref, sems = outs[6:]
     i = pl.program_id(0)
     heads = weights_ref.shape[0]
     chunks = x_refs[0].shape[0] // blk
+
+    def copies():
+        pairs = [(acts_ref, acts_out), (slopes_ref, slopes_out), (gate_ref, gate_out)]
+        if count > 1:
+            for b in range(count):
+                for r in range(chunks):
+                    at = pl.ds(pl.multiple_of(order_ref[b * chunks + r] * blk, blk), blk)
+                    pairs.append((x_refs[b].at[pl.ds(r * blk, blk), :], x_out_ref.at[at, :]))
+        return [pltpu.make_async_copy(source, target, sems.at[n]) for n, (source, target) in enumerate(pairs)]
 
     @pl.when(i == 0)
     def _():
@@ -73,8 +83,6 @@
             for r in range(chunks):
                 at = pl.ds(pl.multiple_of(order_ref[b * chunks + r] * blk, blk), blk)
                 x = x_refs[b][r * blk : (r + 1) * blk, :]
-                if count > 1:
-                    x_out_ref[at, :] = x
                 for p in range(heads // 2):
                     lanes = slice(p * 4 * PAIR, (p + 1) * 4 * PAIR)
                     half = 0.5 * dot_nn(x, w_ref[:, lanes])
@@ -87,6 +95,8 @@
                 for h in range(heads):
                     k_t[h * DH : (h + 1) * DH, at] = jnp.transpose(acts_ref[at, head_columns(2, h)])
                 split_pairs(acts_ref, v_split, 0, order_ref[b * chunks + r], blk)
+        for copy in copies():
+            copy.start()
 
     at_i = pl.ds(pl.multiple_of(i * blk, blk), blk)
     q_half = [acts_ref[at_i, head_columns(1, h)] * jnp.asarray(0.5 * DH**-0.5, BF) for h in range(heads)]
@@ -119,6 +129,11 @@
     acc = lax.fori_loop(first, i + 1, column, (zero,) * (heads // 2))
     heads_ref[...] = (jnp.concatenate(acc, axis=1) * (1.0 / maxlen)).astype(BF)
 
+    @pl.when(i == pl.num_programs(0) - 1)
+    def _():
+        for copy in copies():
+            copy.wait()
+
 
 def forward_attention(lengths, order, x_blocks, w_own, blk, maxlen):
     count = len(x_blocks)
@@ -130,9 +145,9 @@
     elements = heads * positions * positions // 2
     whole = lambda i: (0, 0)
     out_specs = [
-        pl.BlockSpec((positions, 4 * cols), whole),
-        pl.BlockSpec((positions, 4 * cols), whole),
-        pl.BlockSpec((positions, cols), whole),
+        pl.BlockSpec(memory_space=pl.ANY),
+        pl.BlockSpec(memory_space=pl.ANY),
+        pl.BlockSpec(memory_space=pl.ANY),
         pl.BlockSpec((heads, blk, positions), lambda i: (0, i, 0)),
         pl.BlockSpec((heads, blk, positions), lambda i: (0, i, 0)),
         pl.BlockSpec((blk, cols), lambda i: (i, 0)),
@@ -146,7 +161,7 @@
         jax.ShapeDtypeStruct((positions, cols), BF),
     ]
     if count > 1:
-        out_specs = [pl.BlockSpec((positions, D), whole)] + out_specs
+        out_specs = [pl.BlockSpec(memory_space=pl.ANY)] + out_specs
         out_shape = [jax.ShapeDtypeStruct((positions, D), BF)] + out_shape
     return pl.pallas_call(
         functools.partial(forward_kernel, blk=blk, users=users, maxlen=maxlen, count=count),
@@ -156,7 +171,14 @@
         + [pl.BlockSpec((D, 4 * cols), whole)],
         out_specs=out_specs,
         out_shape=out_shape,
-        scratch_shapes=[pltpu.VMEM((cols, positions), BF), pltpu.VMEM((cols // PAIR, 2 * positions, PAIR), BF)],
+        scratch_shapes=[
+            pltpu.VMEM((cols, positions), BF),
+            pltpu.VMEM((cols // PAIR, 2 * positions, PAIR), BF),
+            pltpu.VMEM((positions, 4 * cols), BF),
+            pltpu.VMEM((positions, 4 * cols), BF),
+            pltpu.VMEM((positions, cols), F32),
+            pltpu.SemaphoreType.DMA((3 + positions // blk,)),
+        ],
         compiler_params=pltpu.CompilerParams(vmem_limit_bytes=VMEM_LIMIT),
         cost_estimate=pl.CostEstimate(
             flops=8 * positions * D * cols + 4 * elements * 256,
@@ -167,49 +189,62 @@
     )(lengths, order, *x_blocks, w_own)
 
 
-def stats_kernel(*refs, blk, count):
-    order_ref = refs[0]
+def stats_kernel(*refs, count):
     og_refs = refs[1 : 1 + count]
     w_ref, gate_ref, heads_ref = refs[1 + count : 4 + count]
     outs = refs[4 + count :]
+    og = og_refs[0][...]
     if count > 1:
         og_out_ref, outs = outs[0], outs[1:]
+        chunks = pl.num_programs(0) // count
+        for b in range(1, count):
+            og = jnp.where(pl.program_id(0) >= b * chunks, og_refs[b][...], og)
+        og_out_ref[...] = og
     mg_ref, stats_ref = outs
-    chunks = og_refs[0].shape[0] // blk
-    for b in range(count):
-        for r in range(chunks):
-            at = pl.ds(pl.multiple_of(order_ref[b * chunks + r] * blk, blk), blk)
-            og = og_refs[b][r * blk : (r + 1) * blk, :]
-            if count > 1:
-                og_out_ref[at, :] = og
-            mg = dot_nt(og, w_ref[...])
-            mg_ref[at, :] = mg
-            ng = mg * gate_ref[at, :]
-            heads = heads_ref[at, :].astype(F32)
-            mean = jnp.mean(heads, axis=1, keepdims=True)
-            centred = heads - mean
-            square = jnp.sum(centred * centred, axis=1, keepdims=True)
-            total = jnp.sum(ng, axis=1, keepdims=True)
-            cross = jnp.sum(ng * centred, axis=1, keepdims=True)
-            lane = lax.broadcasted_iota(jnp.int32, (blk, 128), 1)
-            packed = jnp.where(lane == 0, mean, jnp.where(lane == 1, square, jnp.where(lane == 2, total, cross)))
-            stats_ref[:, at] = jnp.transpose(packed)[:8, :]
+    mg = dot_nt(og, w_ref[...])
+    mg_ref[...] = mg
+    ng = mg * gate_ref[...]
+    heads = heads_ref[...].astype(F32)
+    mean = jnp.mean(heads, axis=1, keepdims=True)
+    centred = heads - mean
+    square = jnp.sum(centred * centred, axis=1, keepdims=True)
+    total = jnp.sum(ng, axis=1, keepdims=True)
+    cross = jnp.sum(ng * centred, axis=1, keepdims=True)
+    lane = lax.broadcasted_iota(jnp.int32, (heads.shape[0], 128), 1)
+    packed = jnp.where(lane == 0, mean, jnp.where(lane == 1, square, jnp.where(lane == 2, total, cross)))
+    stats_ref[...] = jnp.transpose(packed)[:8, :]
 
 
 def event_stats(order, og_blocks, w_out_own, gate, heads, blk):
     positions, cols = heads.shape
     count = len(og_blocks)
-    vmem = pl.BlockSpec(memory_space=pltpu.VMEM)
+    steps = positions // blk
+    chunks = steps // count
+    placed = lambda i, order: (order[i], 0)
+    og_specs = [
+        pl.BlockSpec((blk, D), lambda i, order, b=b: (jnp.clip(i - b * chunks, 0, chunks - 1), 0)) for b in range(count)
+    ]
+    out_specs = [pl.BlockSpec((blk, cols), placed), pl.BlockSpec((8, blk), lambda i, order: (0, order[i]))]
     out_shape = [
         jax.ShapeDtypeStruct((positions, cols), F32),
         jax.ShapeDtypeStruct((8, positions), F32),
     ]
     if count > 1:
+        out_specs = [pl.BlockSpec((blk, D), placed)] + out_specs
         out_shape = [jax.ShapeDtypeStruct((positions, D), BF)] + out_shape
     return pl.pallas_call(
-        functools.partial(stats_kernel, blk=blk, count=count),
-        in_specs=[pl.BlockSpec(memory_space=pltpu.SMEM)] + [vmem] * (count + 3),
-        out_specs=[vmem] * len(out_shape),
+        functools.partial(stats_kernel, count=count),
+        grid_spec=pltpu.PrefetchScalarGridSpec(
+            num_scalar_prefetch=1,
+            grid=(steps,),
+            in_specs=og_specs
+            + [
+                pl.BlockSpec((cols, D), lambda i, order: (0, 0)),
+                pl.BlockSpec((blk, cols), placed),
+                pl.BlockSpec((blk, cols), placed),
+            ],
+            out_specs=out_specs,
+        ),
         out_shape=out_shape,
         compiler_params=pltpu.CompilerParams(vmem_limit_bytes=VMEM_LIMIT),
         cost_estimate=pl.CostEstimate(

time: 173 us -> 175 us (1.012)
  transfers between devices with their start and end apart: 22 -> 22, of which waited for: 9 -> 9; matrix products, arithmetic and copies ran while one was open for 15% -> 15% of each run, Pallas kernels for 10% -> 9%
where the time goes in v1:
time: 175 us; the launch traced here: 174 us
  starting transfers between devices  59.8 us (34%)
  Pallas kernels  42.1 us (24%)
  waiting for transfers between devices  35.9 us (21%)
  matrix products  14.1 us (8%)
  local copies, waits for them, and re-layouts  10.8 us (6%)
  other arithmetic  10.6 us (6%)
    ppermute x21, starting transfers between devices, send(): return lax.ppermute(array, ('seq', 'dp'), steps)  55 us
    ppermute x21, waiting for transfers between devices, send(): return lax.ppermute(array, ('seq', 'dp'), steps)  35.9 us
    pallas_call x1, Pallas kernels, backward_attention(): pl.pallas_call(functools.partial(backward_kernel, blk=blk, users=users, m...  16.1 us
    pallas_call x1, Pallas kernels, forward_attention(): pl.pallas_call(functools.partial(forward_kernel, blk=blk, users=users, ma...  16 us
    dot_general x4, matrix products, dot_nt(): lax.dot_general(a, b, (((1,), (1,)), ((), ())), preferred_element_type=F32)  8.4 us
    pallas_call x1, Pallas kernels, event_stats(): pl.pallas_call(functools.partial(stats_kernel, count=count), grid_spec=pl...  5.85 us
    all_to_all x1, starting transfers between devices, rows_to_owners(): lax.all_to_all(rows.reshape(devices, capacity, D + 128), ('seq', 'dp'), s...  4.82 us
    pallas_call x1, Pallas kernels, update_rows(): pl.pallas_call(update_kernel, grid=(rows_own // blk,), in_specs=[pl.Block...  4.19 us
  transfers between devices with their start and end apart: 22, of which 9 were waited for; matrix products, arithmetic and copies ran while one was open for 15% of the time, Pallas kernels for 9%

profile of v1, /device:TPU:0, one launch (start us, length us, event | category | flops | bytes accessed | tf_op | source)
XLA Modules:
  0.0 174.4 jit_solution(9173511161245659888)
XLA Ops:
  1.5 3.1 %collective-permute-start.1 = (bf16[256,1024]{1,0:T(8,128)(2,1)}, bf16[256,1024]{1,0:T(8,128)(2,1)S(1)}, u32[]{:S(2)}, u32[]{:S(2)}) collective-permute-start(bf16[256,1024]{1,0:T(8,128)(2,1)} %param.10), channel_id=1, source_target_pairs={{0,8},{1,16},{2,10},{3,18},{4,12},{5,20},{6,14},{7,22},{8,0},{9,24... | collective-permute-start | bytes 1572872 | tf_op jit(solution)/shard_map/ppermute | solution.py:549
  9.2 1.5 constant_dynamic-slice_fusion.6
  10.8 1.6 pad_maximum_fusion.refs_4_
  14.7 16.3 %collective-permute-start.3 = (bf16[512,1024]{1,0:T(8,128)(2,1)S(1)}, bf16[512,1024]{1,0:T(8,128)(2,1)}, u32[]{:S(2)}, u32[]{:S(2)}) collective-permute-start(bf16[512,1024]{1,0:T(8,128)(2,1)S(1)} %pad_maximum_fusion.1.refs_2_), channel_id=1, source_target_pairs={{0,1},{1,0},{2,3},{3,2},{4,5},{5,4},{6,7},{7,6},{8,9},{9,8},{10,11... | collective-permute-start | bytes 3145736 | tf_op jit(solution)/shard_map/ppermute | solution.py:549
  31.7 1.7 collective-permute-start.5
  34.0 16.0 %attention_forward.1 = (bf16[1024,1024]{1,0:T(8,128)(2,1)}, bf16[1024,1024]{1,0:T(8,128)(2,1)}, bf16[1024,1024]{1,0:T(8,128)(2,1)}, f32[1024,256]{1,0:T(8,128)},...) custom-call(s32[1,3]{1,0:T(1,128)} %slice.47.refs_0_, ...), custom_call_target="tpu_custom_call" | custom-call | flops 4294967296 | bytes 12582912 | tf_op jit(solution)/shard_map/attention_forward/pallas_call | solution.py:166
  50.2 9.5 %collective-permute-start.6 = (bf16[512,1024]{1,0:T(8,128)(2,1)S(1)}, bf16[512,1024]{1,0:T(8,128)(2,1)S(1)}, u32[]{:S(2)}, u32[]{:S(2)}) collective-permute-start(bf16[512,1024]{1,0:T(8,128)(2,1)S(1)} %pad_maximum_fusion.2.refs_1_), channel_id=1, source_target_pairs={{0,1},{1,0},{2,3},{3,2},{4,5},{5,4},{6,7},{7,6},{8,9},{9,8},{10,11... | collective-permute-start | bytes 3145736 | tf_op jit(solution)/shard_map/ppermute | solution.py:549
  59.7 2.3 %collective-permute-done.6.refs_2_ = bf16[512,1024]{1,0:T(8,128)(2,1)S(1)} collective-permute-done((bf16[512,1024]{1,0:T(8,128)(2,1)S(1)}, bf16[512,1024]{1,0:T(8,128)(2,1)S(1)}, u32[]{:S(2)}, u32[]{:S(2)}) %collective-permute-start.6) | collective-permute-done | bytes 1048608 | tf_op jit(solution)/shard_map/ppermute | solution.py:549
  62.9 5.9 %event_stats.1 = (bf16[1024,1024]{1,0:T(8,128)(2,1)}, f32[1024,256]{1,0:T(8,128)}, f32[8,1024]{1,0:T(8,128)}) custom-call(s32[4]{0:T(128)} %pad_add_fusion.1.refs_1_.refs_0_, bf16[512,1024]{1,0:T(8,128)(2,1)} %copy-done.3, bf16[512,1024]{1,0:T(8,128)(2,1)} %copy-done.8, bf16[256,1024]{1,0:T(8,128)(2,1)} %constant_dynamic-slice_fusion.2.refs_3_, ...), custom_call_target="tpu_custom_call" | custom-call | flops 536870912 | bytes 6815744 | tf_op jit(solution)/shard_map/event_stats/pallas_call | solution.py:235
  69.2 1.5 collective-permute-start.9
  70.6 2.6 %collective-permute-done.8.refs_3_ = f32[8,1024]{1,0:T(8,128)S(1)} collective-permute-done((f32[8,1024]{1,0:T(8,128)}, f32[8,1024]{1,0:T(8,128)S(1)}, u32[]{:S(2)}, u32[]{:S(2)}) %collective-permute-start.8) | collective-permute-done | bytes 32800 | tf_op jit(solution)/shard_map/ppermute | solution.py:549
  73.9 16.1 %attention_backward.1 = (bf16[1024,1024]{1,0:T(8,128)(2,1)}, bf16[1024,256]{1,0:T(8,128)(2,1)}) custom-call(s32[1,3]{1,0:T(1,128)} %slice.47.refs_0_, f32[8,1024]{1,0:T(8,128)} %get-tuple-element.48.refs_1_, f32[8,1024]{1,0:T(8,128)} %copy-done.13, f32[8,1024]{1,0:T(8,128)} %copy-done.14, f32[8,1024]{1,0:T(8,128)} %copy-done.15, ...), custom_call_target="tpu_custom_call" | custom-call | flops 4294967296 | bytes 15204352 | tf_op jit(solution)/shard_map/attention_backward/pallas_call | solution.py:353
  90.0 1.8 %convolution_convert_fusion.4 = bf16[256,1024]{1,0:T(8,128)(2,1)S(1)} fusion(bf16[1024,1024]{1,0:T(8,128)(2,1)S(1)} %copy-done.5, bf16[1024,1024]{1,0:T(8,128)(2,1)} %get-tuple-element.57, s32[]{:T(128)S(6)} %select_n.201), kind=kOutput, calls=%fused_computation.12 | convolution fusion | flops 537133056 | bytes 3145732 | tf_op jit(solution)/shard_map/dot_general | solution.py:27
  92.0 1.9 %collective-permute-done.10 = bf16[256,1024]{1,0:T(8,128)(2,1)} collective-permute-done((bf16[256,1024]{1,0:T(8,128)(2,1)S(1)}, bf16[256,1024]{1,0:T(8,128)(2,1)}, u32[]{:S(2)}, u32[]{:S(2)}) %collective-permute-start.10) | collective-permute-done | bytes 524320 | tf_op jit(solution)/shard_map/ppermute | solution.py:549
  93.9 2.7 %fusion.3 = bf16[256,1024]{1,0:T(8,128)(2,1)} fusion(bf16[1024,1024]{1,0:T(8,128)(2,1)S(1)} %copy-done.5, bf16[256,1024]{1,0:T(8,128)(2,1)} %collective-permute-done.10, bf16[1024,1024]{1,0:T(8,128)(2,1)} %get-tuple-element.57, s32[]{:T(128)S(6)} %select_n.200), kind=kOutput, calls=%fused_computation.13 | convolution fusion | flops 537657344 | bytes 3670020 | tf_op jit(solution)/shard_map/dot_general | solution.py:27
  96.6 1.6 convolution_convert_fusion.3
  98.4 1.8 %collective-permute-start.20 = (bf16[256,1024]{1,0:T(8,128)(2,1)}, bf16[256,1024]{1,0:T(8,128)(2,1)}, u32[]{:S(2)}, u32[]{:S(2)}) collective-permute-start(bf16[256,1024]{1,0:T(8,128)(2,1)} %fusion.3), channel_id=1, source_target_pairs={{0,8},{1,9},{2,10},{3,11},{4,12},{5,13},{6,14},{7,15},{8,0},{9,1},... | collective-permute-start | bytes 1572872 | tf_op jit(solution)/shard_map/ppermute | solution.py:549
  100.2 2.4 %convolution_convert_fusion.1 = bf16[1024,1024]{1,0:T(8,128)(2,1)S(1)} fusion(bf16[1024,1024]{1,0:T(8,128)(2,1)S(1)} %copy-done.18, bf16[1024,1024]{1,0:T(8,128)(2,1)S(1)} %copy-done.17), kind=kOutput, calls=%fused_computation.2 | convolution fusion | flops 2148532224 | bytes 6291456 | tf_op jit(solution)/shard_map/dot_general | solution.py:480
  102.6 1.5 convolution_convert_fusion.2
  104.4 1.4 reshape.171
  110.3 1.7 collective-permute-start.11
  112.9 2.3 %fusion.4 = bf16[256,1024]{1,0:T(8,128)(2,1)S(1)} fusion(bf16[1024,1024]{1,0:T(8,128)(2,1)S(1)} %copy-done.6, bf16[256,1024]{1,0:T(8,128)(2,1)} %collective-permute-done.20, bf16[256,1024]{1,0:T(8,128)(2,1)} %collective-permute-done.19, bf16[256,1024]{1,0:T(8,128)(2,1)S(1)} %broadcast_select_fusion, bf16[1024,1024]{1,0:T(8,128)(2,1)} %get-tuple-element.57, ...), kind=kOutput, calls=%fused_computation.14 | convolution fusion | flops 538705920 | bytes 4718596 | tf_op jit(solution)/shard_map/dot_general | solution.py:27
  115.2 1.5 convolution_convert_fusion
  116.7 4.8 %all-to-all-start = ((bf16[32,16,1152]{2,1,0:T(8,128)(2,1)}), bf16[32,16,1152]{2,1,0:T(8,128)(2,1)S(1)}, u32[]{:S(2)}, u32[]{:S(2)}) async-start(bf16[32,16,1152]{2,1,0:T(8,128)(2,1)} %bitcast.28), calls=%async_computation | async-start | bytes 2359296 | tf_op jit(solution)/shard_map/all_to_all | solution.py:470
  121.6 3.9 %collective-permute-done.13 = bf16[2,256,640]{2,1,0:T(8,128)(2,1)} collective-permute-done((bf16[2,256,640]{2,1,0:T(8,128)(2,1)}, bf16[2,256,640]{2,1,0:T(8,128)(2,1)}, u32[]{:S(2)}, u32[]{:S(2)}) %collective-permute-start.13) | collective-permute-done | bytes 655392 | tf_op jit(solution)/shard_map/ppermute | solution.py:549
  126.8 3.6 %collective-permute-start.14 = (bf16[256,640]{1,0:T(8,128)(2,1)S(1)}, bf16[256,640]{1,0:T(8,128)(2,1)S(1)}, u32[]{:S(2)}, u32[]{:S(2)}) collective-permute-start(bf16[256,640]{1,0:T(8,128)(2,1)S(1)} %dynamic-slice_bitcast_fusion.3), channel_id=1, source_target_pairs={{0,2},{1,3},{2,0},{3,1},{4,6},{5,7},{6,4},{7,5},{8,10},{9,11},{10,... | collective-permute-start | bytes 983048 | tf_op jit(solution)/shard_map/ppermute | solution.py:549
  130.4 1.5 collective-permute-done.11
  134.3 10.8 %collective-permute-done.14 = bf16[256,640]{1,0:T(8,128)(2,1)S(1)} collective-permute-done((bf16[256,640]{1,0:T(8,128)(2,1)S(1)}, bf16[256,640]{1,0:T(8,128)(2,1)S(1)}, u32[]{:S(2)}, u32[]{:S(2)}) %collective-permute-start.14) | collective-permute-done | bytes 327712 | tf_op jit(solution)/shard_map/ppermute | solution.py:549
  145.9 3.1 %collective-permute-start.18 = (bf16[128,256]{1,0:T(8,128)(2,1)S(1)}, bf16[128,256]{1,0:T(8,128)(2,1)S(1)}, u32[]{:S(2)}, u32[]{:S(2)}) collective-permute-start(bf16[128,256]{1,0:T(8,128)(2,1)S(1)} %get-tuple-element.82), channel_id=1, source_target_pairs={{0,1},{1,3},{2,9},{3,11},{4,17},{5,19},{6,25},{7,27},{8,5},{9,7},{... | collective-permute-start | bytes 196616 | tf_op jit(solution)/shard_map/ppermute | solution.py:549
  149.9 6.0 %collective-permute-start.16 = (bf16[128,1024]{1,0:T(8,128)(2,1)S(1)}, bf16[128,1024]{1,0:T(8,128)(2,1)S(1)}, u32[]{:S(2)}, u32[]{:S(2)}) collective-permute-start(bf16[128,1024]{1,0:T(8,128)(2,1)S(1)} %get-tuple-element.78), channel_id=1, source_target_pairs={{0,1},{1,9},{2,3},{3,11},{4,5},{5,13},{6,7},{7,15},{8,17},{9,25},{... | collective-permute-start | bytes 786440 | tf_op jit(solution)/shard_map/ppermute | solution.py:549
  156.6 11.0 %collective-permute-done.16 = bf16[128,1024]{1,0:T(8,128)(2,1)S(1)} collective-permute-done((bf16[128,1024]{1,0:T(8,128)(2,1)S(1)}, bf16[128,1024]{1,0:T(8,128)(2,1)S(1)}, u32[]{:S(2)}, u32[]{:S(2)}) %collective-permute-start.16) | collective-permute-done | bytes 262176 | tf_op jit(solution)/shard_map/ppermute | solution.py:549
  170.2 4.2 %update_rows.1 = (f32[512,1024]{1,0:T(8,128)}, f32[1,512]{1,0:T(1,128)}) custom-call(bf16[512,1152]{1,0:T(8,128)(2,1)} %bitcast.62, f32[512,1024]{1,0:T(8,128)} %table_ref.1, f32[1,512]{1,0:T(1,128)} %bitcast.75), custom_call_target="tpu_custom_call" | custom-call | flops 536870912 | bytes 5242880 | tf_op jit(solution)/shard_map/update_rows/pallas_call | solution.py:412
  (110 shorter events, 25.7 us)
Async XLA Ops:
  0.6 6.7 %copy-start = (bf16[1024,1024]{1,0:T(8,128)(2,1)S(1)}, bf16[1024,1024]{1,0:T(8,128)(2,1)}, u32[]{:S(2)}) copy-start(bf16[1024,1024]{1,0:T(8,128)(2,1)} %param.17) | copy-start | bytes 6291460
  0.6 12.8 %collective-permute-start = (bf16[256,1024]{1,0:T(8,128)(2,1)}, bf16[256,1024]{1,0:T(8,128)(2,1)S(1)}, u32[]{:S(2)}, u32[]{:S(2)}) collective-permute-start(bf16[256,1024]{1,0:T(8,128)(2,1)} %param.10), channel_id=1, source_target_pairs={{1,24},{3,26},{5,28},{7,30},{9,16},{11,18},{13,20},{15,22},{16,9},... | collective-permute-start | bytes 1572872 | tf_op jit(solution)/shard_map/ppermute | solution.py:549
  1.5 13.1 %collective-permute-start.1 = (bf16[256,1024]{1,0:T(8,128)(2,1)}, bf16[256,1024]{1,0:T(8,128)(2,1)S(1)}, u32[]{:S(2)}, u32[]{:S(2)}) collective-permute-start(bf16[256,1024]{1,0:T(8,128)(2,1)} %param.10), channel_id=1, source_target_pairs={{0,8},{1,16},{2,10},{3,18},{4,12},{5,20},{6,14},{7,22},{8,0},{9,24... | collective-permute-start | bytes 1572872 | tf_op jit(solution)/shard_map/ppermute | solution.py:549
  6.6 5.8 %collective-permute-start.2 = (s32[1,384]{1,0:T(1,128)S(1)}, s32[1,384]{1,0:T(1,128)S(1)}, u32[]{:S(2)}, u32[]{:S(2)}) collective-permute-start(s32[1,384]{1,0:T(1,128)S(1)} %pad_add_fusion), channel_id=1, source_target_pairs={{1,24},{3,26},{5,28},{7,30},{9,16},{11,18},{13,20},{15,22},{16,9},... | collective-permute-start | bytes 4616 | tf_op jit(solution)/shard_map/ppermute | solution.py:549
  10.8 3.8 %copy-start.10 = (bf16[256,1024]{1,0:T(8,128)(2,1)S(1)}, bf16[256,1024]{1,0:T(8,128)(2,1)}, u32[]{:S(2)}) copy-start(bf16[256,1024]{1,0:T(8,128)(2,1)} %param.10) | copy-start | bytes 1572868
  12.4 18.6 %copy-start.11 = (bf16[256,1024]{1,0:T(8,128)(2,1)S(1)}, bf16[256,1024]{1,0:T(8,128)(2,1)}, u32[]{:S(2)}) copy-start(bf16[256,1024]{1,0:T(8,128)(2,1)} %param.11) | copy-start | bytes 1572868
  14.7 19.3 %copy-start.9 = (bf16[512,1024]{1,0:T(8,128)(2,1)}, bf16[512,1024]{1,0:T(8,128)(2,1)S(1)}, u32[]{:S(2)}) copy-start(bf16[512,1024]{1,0:T(8,128)(2,1)S(1)} %pad_maximum_fusion.1.refs_2_) | copy-start | bytes 3145732
  14.7 19.3 %collective-permute-start.3 = (bf16[512,1024]{1,0:T(8,128)(2,1)S(1)}, bf16[512,1024]{1,0:T(8,128)(2,1)}, u32[]{:S(2)}, u32[]{:S(2)}) collective-permute-start(bf16[512,1024]{1,0:T(8,128)(2,1)S(1)} %pad_maximum_fusion.1.refs_2_), channel_id=1, source_target_pairs={{0,1},{1,0},{2,3},{3,2},{4,5},{5,4},{6,7},{7,6},{8,9},{9,8},{10,11... | collective-permute-start | bytes 3145736 | tf_op jit(solution)/shard_map/ppermute | solution.py:549
  31.0 19.0 %collective-permute-start.4 = (bf16[256,1024]{1,0:T(8,128)(2,1)S(1)}, bf16[256,1024]{1,0:T(8,128)(2,1)S(1)}, u32[]{:S(2)}, u32[]{:S(2)}) collective-permute-start(bf16[256,1024]{1,0:T(8,128)(2,1)S(1)} %copy-done.11), channel_id=1, source_target_pairs={{1,24},{3,26},{5,28},{7,30},{9,16},{11,18},{13,20},{15,22},{16,9},... | collective-permute-start | bytes 1572872 | tf_op jit(solution)/shard_map/ppermute | solution.py:549
  31.7 18.3 %collective-permute-start.5 = (bf16[256,1024]{1,0:T(8,128)(2,1)S(1)}, bf16[256,1024]{1,0:T(8,128)(2,1)S(1)}, u32[]{:S(2)}, u32[]{:S(2)}) collective-permute-start(bf16[256,1024]{1,0:T(8,128)(2,1)S(1)} %copy-done.11), channel_id=1, source_target_pairs={{0,8},{1,16},{2,10},{3,18},{4,12},{5,20},{6,14},{7,22},{8,0},{9,24... | collective-permute-start | bytes 1572872 | tf_op jit(solution)/shard_map/ppermute | solution.py:549
  50.2 11.8 %copy-start.3 = (bf16[512,1024]{1,0:T(8,128)(2,1)}, bf16[512,1024]{1,0:T(8,128)(2,1)S(1)}, u32[]{:S(2)}) copy-start(bf16[512,1024]{1,0:T(8,128)(2,1)S(1)} %pad_maximum_fusion.2.refs_1_) | copy-start | bytes 3145732
  50.2 11.8 %collective-permute-start.6 = (bf16[512,1024]{1,0:T(8,128)(2,1)S(1)}, bf16[512,1024]{1,0:T(8,128)(2,1)S(1)}, u32[]{:S(2)}, u32[]{:S(2)}) collective-permute-start(bf16[512,1024]{1,0:T(8,128)(2,1)S(1)} %pad_maximum_fusion.2.refs_1_), channel_id=1, source_target_pairs={{0,1},{1,0},{2,3},{3,2},{4,5},{5,4},{6,7},{7,6},{8,9},{9,8},{10,11... | collective-permute-start | bytes 3145736 | tf_op jit(solution)/shard_map/ppermute | solution.py:549
  68.8 1.9 %collective-permute-start.7 = (f32[8,1024]{1,0:T(8,128)}, f32[8,1024]{1,0:T(8,128)S(1)}, u32[]{:S(2)}, u32[]{:S(2)}) collective-permute-start(f32[8,1024]{1,0:T(8,128)} %get-tuple-element.48.refs_1_), channel_id=1, source_target_pairs={{0,1},{1,0},{2,3},{3,2},{4,5},{5,4},{6,7},{7,6},{8,9},{9,8},{10,11... | collective-permute-start | bytes 98312 | tf_op jit(solution)/shard_map/ppermute | solution.py:549
  69.2 4.1 %collective-permute-start.8 = (f32[8,1024]{1,0:T(8,128)}, f32[8,1024]{1,0:T(8,128)S(1)}, u32[]{:S(2)}, u32[]{:S(2)}) collective-permute-start(f32[8,1024]{1,0:T(8,128)} %get-tuple-element.48.refs_1_), channel_id=1, source_target_pairs={{0,8},{1,9},{2,10},{3,11},{4,12},{5,13},{6,14},{7,15},{8,0},{9,1},... | collective-permute-start | bytes 98312 | tf_op jit(solution)/shard_map/ppermute | solution.py:549
  69.2 4.1 %collective-permute-start.9 = (f32[8,1024]{1,0:T(8,128)}, f32[8,1024]{1,0:T(8,128)S(1)}, u32[]{:S(2)}, u32[]{:S(2)}) collective-permute-start(f32[8,1024]{1,0:T(8,128)} %get-tuple-element.48.refs_1_), channel_id=1, source_target_pairs={{0,9},{1,8},{2,11},{3,10},{4,13},{5,12},{6,15},{7,14},{8,1},{9,0},... | collective-permute-start | bytes 98312 | tf_op jit(solution)/shard_map/ppermute | solution.py:549
  73.9 16.1 %copy-start.5 = (bf16[1024,1024]{1,0:T(8,128)(2,1)S(1)}, bf16[1024,1024]{1,0:T(8,128)(2,1)}, u32[]{:S(2)}) copy-start(bf16[1024,1024]{1,0:T(8,128)(2,1)} %pad_maximum_fusion.refs_4_) | copy-start | bytes 6291460
  91.8 2.1 %collective-permute-start.10 = (bf16[256,1024]{1,0:T(8,128)(2,1)S(1)}, bf16[256,1024]{1,0:T(8,128)(2,1)}, u32[]{:S(2)}, u32[]{:S(2)}) collective-permute-start(bf16[256,1024]{1,0:T(8,128)(2,1)S(1)} %convolution_convert_fusion.4), channel_id=1, source_target_pairs={{0,1},{1,0},{2,3},{3,2},{4,5},{5,4},{6,7},{7,6},{8,9},{9,8},{10,11... | collective-permute-start | bytes 1572872 | tf_op jit(solution)/shard_map/ppermute | solution.py:549
  92.0 4.6 %copy-start.17 = (bf16[1024,1024]{1,0:T(8,128)(2,1)S(1)}, bf16[1024,1024]{1,0:T(8,128)(2,1)}, u32[]{:S(2)}) copy-start(bf16[1024,1024]{1,0:T(8,128)(2,1)} %get-tuple-element.57) | copy-start | bytes 6291460
  98.2 13.8 %collective-permute-start.19 = (bf16[256,1024]{1,0:T(8,128)(2,1)}, bf16[256,1024]{1,0:T(8,128)(2,1)}, u32[]{:S(2)}, u32[]{:S(2)}) collective-permute-start(bf16[256,1024]{1,0:T(8,128)(2,1)} %convolution_convert_fusion.3), channel_id=1, source_target_pairs={{0,1},{1,0},{2,3},{3,2},{4,5},{5,4},{6,7},{7,6},{8,9},{9,8},{10,11... | collective-permute-start | bytes 1572872 | tf_op jit(solution)/shard_map/ppermute | solution.py:549
  98.4 14.5 %collective-permute-start.20 = (bf16[256,1024]{1,0:T(8,128)(2,1)}, bf16[256,1024]{1,0:T(8,128)(2,1)}, u32[]{:S(2)}, u32[]{:S(2)}) collective-permute-start(bf16[256,1024]{1,0:T(8,128)(2,1)} %fusion.3), channel_id=1, source_target_pairs={{0,8},{1,9},{2,10},{3,11},{4,12},{5,13},{6,14},{7,15},{8,0},{9,1},... | collective-permute-start | bytes 1572872 | tf_op jit(solution)/shard_map/ppermute | solution.py:549
  106.2 6.7 %copy-start.6 = (bf16[1024,1024]{1,0:T(8,128)(2,1)S(1)}, bf16[1024,1024]{1,0:T(8,128)(2,1)}, u32[]{:S(2)}) copy-start(bf16[1024,1024]{1,0:T(8,128)(2,1)} %pad_maximum_fusion.refs_4_) | copy-start | bytes 6291460
  108.0 17.5 %collective-permute-start.13 = (bf16[2,256,640]{2,1,0:T(8,128)(2,1)}, bf16[2,256,640]{2,1,0:T(8,128)(2,1)}, u32[]{:S(2)}, u32[]{:S(2)}) collective-permute-start(bf16[2,256,640]{2,1,0:T(8,128)(2,1)} %pad_maximum_fusion.3), channel_id=1, source_target_pairs={{0,4},{1,5},{2,6},{3,7},{4,0},{5,1},{6,2},{7,3},{8,12},{9,13},{10,... | collective-permute-start | bytes 1966088 | tf_op jit(solution)/shard_map/ppermute | solution.py:549
  110.3 21.6 %collective-permute-start.11 = (bf16[2,256,640]{2,1,0:T(8,128)(2,1)}, bf16[2,256,640]{2,1,0:T(8,128)(2,1)}, u32[]{:S(2)}, u32[]{:S(2)}) collective-permute-start(bf16[2,256,640]{2,1,0:T(8,128)(2,1)} %dynamic-slice_bitcast_fusion), channel_id=1, source_target_pairs={{0,2},{1,3},{2,0},{3,1},{4,6},{5,7},{6,4},{7,5},{8,10},{9,11},{10,... | collective-permute-start | bytes 1966088 | tf_op jit(solution)/shard_map/ppermute | solution.py:549
  115.2 10.3 %copy-start.7 = (bf16[2,256,384]{2,1,0:T(8,128)(2,1)S(1)}, bf16[2,256,384]{2,1,0:T(8,128)(2,1)}, u32[]{:S(2)}) copy-start(bf16[2,256,384]{2,1,0:T(8,128)(2,1)} %get-tuple-element.71) | copy-start | bytes 1179652
  116.7 52.4 %all-to-all-start = ((bf16[32,16,1152]{2,1,0:T(8,128)(2,1)}), bf16[32,16,1152]{2,1,0:T(8,128)(2,1)S(1)}, u32[]{:S(2)}, u32[]{:S(2)}) async-start(bf16[32,16,1152]{2,1,0:T(8,128)(2,1)} %bitcast.28), calls=%async_computation | async-start | bytes 2359296 | tf_op jit(solution)/shard_map/all_to_all | solution.py:470
  126.8 18.3 %collective-permute-start.14 = (bf16[256,640]{1,0:T(8,128)(2,1)S(1)}, bf16[256,640]{1,0:T(8,128)(2,1)S(1)}, u32[]{:S(2)}, u32[]{:S(2)}) collective-permute-start(bf16[256,640]{1,0:T(8,128)(2,1)S(1)} %dynamic-slice_bitcast_fusion.3), channel_id=1, source_target_pairs={{0,2},{1,3},{2,0},{3,1},{4,6},{5,7},{6,4},{7,5},{8,10},{9,11},{10,... | collective-permute-start | bytes 983048 | tf_op jit(solution)/shard_map/ppermute | solution.py:549
  133.2 15.8 %collective-permute-start.12 = (bf16[256,640]{1,0:T(8,128)(2,1)S(1)}, bf16[256,640]{1,0:T(8,128)(2,1)S(1)}, u32[]{:S(2)}, u32[]{:S(2)}) collective-permute-start(bf16[256,640]{1,0:T(8,128)(2,1)S(1)} %dynamic-slice_bitcast_fusion.4), channel_id=1, source_target_pairs={{0,4},{1,5},{2,6},{3,7},{4,0},{5,1},{6,2},{7,3},{8,12},{9,13},{10,... | collective-permute-start | bytes 983048 | tf_op jit(solution)/shard_map/ppermute | solution.py:549
  145.3 10.6 %collective-permute-start.17 = (bf16[128,256]{1,0:T(8,128)(2,1)S(1)}, bf16[128,256]{1,0:T(8,128)(2,1)S(1)}, u32[]{:S(2)}, u32[]{:S(2)}) collective-permute-start(bf16[128,256]{1,0:T(8,128)(2,1)S(1)} %get-tuple-element.81), channel_id=1, source_target_pairs={{0,0},{1,2},{2,8},{3,10},{4,16},{5,18},{6,24},{7,26},{8,4},{9,6},{... | collective-permute-start | bytes 196616 | tf_op jit(solution)/shard_map/ppermute | solution.py:549
  145.9 9.9 %collective-permute-start.18 = (bf16[128,256]{1,0:T(8,128)(2,1)S(1)}, bf16[128,256]{1,0:T(8,128)(2,1)S(1)}, u32[]{:S(2)}, u32[]{:S(2)}) collective-permute-start(bf16[128,256]{1,0:T(8,128)(2,1)S(1)} %get-tuple-element.82), channel_id=1, source_target_pairs={{0,1},{1,3},{2,9},{3,11},{4,17},{5,19},{6,25},{7,27},{8,5},{9,7},{... | collective-permute-start | bytes 196616 | tf_op jit(solution)/shard_map/ppermute | solution.py:549
  149.2 7.3 %collective-permute-start.15 = (bf16[128,1024]{1,0:T(8,128)(2,1)S(1)}, bf16[128,1024]{1,0:T(8,128)(2,1)S(1)}, u32[]{:S(2)}, u32[]{:S(2)}) collective-permute-start(bf16[128,1024]{1,0:T(8,128)(2,1)S(1)} %get-tuple-element.77), channel_id=1, source_target_pairs={{0,0},{1,8},{2,2},{3,10},{4,4},{5,12},{6,6},{7,14},{8,16},{9,24},{... | collective-permute-start | bytes 786440 | tf_op jit(solution)/shard_map/ppermute | solution.py:549
  149.9 17.6 %collective-permute-start.16 = (bf16[128,1024]{1,0:T(8,128)(2,1)S(1)}, bf16[128,1024]{1,0:T(8,128)(2,1)S(1)}, u32[]{:S(2)}, u32[]{:S(2)}) collective-permute-start(bf16[128,1024]{1,0:T(8,128)(2,1)S(1)} %get-tuple-element.78), channel_id=1, source_target_pairs={{0,1},{1,9},{2,3},{3,11},{4,5},{5,13},{6,7},{7,15},{8,17},{9,25},{... | collective-permute-start | bytes 786440 | tf_op jit(solution)/shard_map/ppermute | solution.py:549
  168.3 6.1 %copy-start.1 = (bf16[1024,1024]{1,0:T(8,128)(2,1)S(1)}, bf16[1024,1024]{1,0:T(8,128)(2,1)}, u32[]{:S(2)}) copy-start(bf16[1024,1024]{1,0:T(8,128)(2,1)} %param.17) | copy-start | bytes 6291460
  (9 other events, 16.0 us)

commit v2 on v0

--- a/solution.py
+++ b/solution.py
@@ -352,45 +352,54 @@
     )(lengths, *stats, mg, gate, head_outs, acts, slopes, weights, score_slope)
 
 
-def update_kernel(rows_ref, table_ref, accum_ref, new_table_ref, new_accum_ref, ids):
-    i = pl.program_id(0)
-    blk = table_ref.shape[0]
+def update_kernel(rows_hbm, table_hbm, accum_ref, new_table_hbm, new_accum_ref, rows_ref, table_ref, new_ref, sems):
     slots = rows_ref.shape[0]
-
-    @pl.when(i == 0)
-    def _():
-        numbers = jnp.transpose(rows_ref[:, D:].astype(F32))
-        ids[...] = (numbers[0:1, :] * 256.0 + numbers[1:2, :]).astype(jnp.int32)
-
-    row = i * blk + lax.broadcasted_iota(jnp.int32, (blk, slots), 0)
-    hits = jnp.where(row == ids[...], 1.0, 0.0).astype(BF)
-    grad = dot_nn(hits, rows_ref[:, :D])
-    accum = jnp.transpose(jnp.broadcast_to(accum_ref[...], (128, blk)))[:, :1] + jnp.mean(grad * grad, axis=1, keepdims=True)
-    new_accum_ref[...] = jnp.transpose(jnp.broadcast_to(accum, (blk, 128)))[:1, :]
-    new_table_ref[...] = table_ref[...] - LEARN_RATE * grad * lax.rsqrt(accum)
+    rows_own = table_ref.shape[0]
+    blk = min(256, rows_own)
+    blocks = [pl.ds(b * blk, blk) for b in range(rows_own // blk)]
+    fetch_rows = pltpu.make_async_copy(rows_hbm, rows_ref, sems.at[0])
+    fetch_rows.start()
+    fetches, stores = [], []
+    for b, at in enumerate(blocks):
+        fetches.append(pltpu.make_async_copy(table_hbm.at[at, :], table_ref.at[at, :], sems.at[1 + 2 * b]))
+        stores.append(pltpu.make_async_copy(new_ref.at[at, :], new_table_hbm.at[at, :], sems.at[2 + 2 * b]))
+        fetches[-1].start()
+    fetch_rows.wait()
+    numbers = jnp.transpose(rows_ref[:, D:].astype(F32))
+    ids = (numbers[0:1, :] * 256.0 + numbers[1:2, :]).astype(jnp.int32)
+    for b, at in enumerate(blocks):
+        row = b * blk + lax.broadcasted_iota(jnp.int32, (blk, slots), 0)
+        hits = jnp.where(row == ids, 1.0, 0.0).astype(BF)
+        grad = dot_nn(hits, rows_ref[:, :D])
+        old = jnp.transpose(jnp.broadcast_to(accum_ref[:, at], (128, blk)))[:, :1]
+        accum = old + jnp.mean(grad * grad, axis=1, keepdims=True)
+        new_accum_ref[:, at] = jnp.transpose(jnp.broadcast_to(accum, (blk, 128)))[:1, :]
+        fetches[b].wait()
+        new_ref[at, :] = table_ref[at, :] - LEARN_RATE * grad * lax.rsqrt(accum)
+        stores[b].start()
+    for store in stores:
+        store.wait()
 
 
 def update_rows(got_rows, emb_table, row_accum):
     rows_own = emb_table.shape[0]
     slots = got_rows.shape[0]
-    blk = min(256, rows_own)
+    hbm = pl.BlockSpec(memory_space=pltpu.HBM)
+    vmem = pl.BlockSpec(memory_space=pltpu.VMEM)
     new_table, new_accum = pl.pallas_call(
         update_kernel,
-        grid=(rows_own // blk,),
-        in_specs=[
-            pl.BlockSpec((slots, D + 128), lambda i: (0, 0)),
-            pl.BlockSpec((blk, D), lambda i: (i, 0)),
-            pl.BlockSpec((1, blk), lambda i: (0, i)),
-        ],
-        out_specs=[
-            pl.BlockSpec((blk, D), lambda i: (i, 0)),
-            pl.BlockSpec((1, blk), lambda i: (0, i)),
-        ],
+        in_specs=[hbm, hbm, vmem],
+        out_specs=[hbm, vmem],
         out_shape=[
             jax.ShapeDtypeStruct((rows_own, D), F32),
             jax.ShapeDtypeStruct((1, rows_own), F32),
         ],
-        scratch_shapes=[pltpu.VMEM((1, slots), jnp.int32)],
+        scratch_shapes=[
+            pltpu.VMEM(got_rows.shape, BF),
+            pltpu.VMEM((rows_own, D), F32),
+            pltpu.VMEM((rows_own, D), F32),
+            pltpu.SemaphoreType.DMA((1 + 2 * (rows_own // min(256, rows_own)),)),
+        ],
         compiler_params=pltpu.CompilerParams(vmem_limit_bytes=VMEM_LIMIT),
         cost_estimate=pl.CostEstimate(
             flops=2 * rows_own * slots * D, bytes_accessed=8 * rows_own * D + 2 * slots * D, transcendentals=rows_own

time: 173 us -> 175 us (1.012)
  starting transfers between devices: 59.9 us -> 63.6 us
  waiting for transfers between devices: 34.7 us -> 31.3 us
    ppermute x21, waiting for transfers between devices: 34.7 us -> 31.3 us  [send(): return lax.ppermute(array, ('seq', 'dp'), steps)]
    ppermute x21, starting transfers between devices: 54.4 us -> 57.3 us  [send(): return lax.ppermute(array, ('seq', 'dp'), steps)]
  transfers between devices with their start and end apart: 22 -> 22, of which waited for: 9 -> 8; matrix products, arithmetic and copies ran while one was open for 15% -> 15% of each run, Pallas kernels for 10% -> 10%
where the time goes in v2:
time: 175 us; the launch traced here: 174 us
  starting transfers between devices  63.6 us (36%)
  Pallas kernels  42.7 us (24%)
  waiting for transfers between devices  31.3 us (18%)
  matrix products  14.1 us (8%)
  local copies, waits for them, and re-layouts  10.8 us (6%)
  other arithmetic  10.6 us (6%)
    ppermute x21, starting transfers between devices, send(): return lax.ppermute(array, ('seq', 'dp'), steps)  57.3 us
    ppermute x21, waiting for transfers between devices, send(): return lax.ppermute(array, ('seq', 'dp'), steps)  31.3 us
    pallas_call x1, Pallas kernels, forward_attention(): pl.pallas_call(functools.partial(forward_kernel, blk=blk, users=users, ma...  16.9 us
    pallas_call x1, Pallas kernels, backward_attention(): pl.pallas_call(functools.partial(backward_kernel, blk=blk, users=users, m...  16.1 us
    dot_general x4, matrix products, dot_nt(): lax.dot_general(a, b, (((1,), (1,)), ((), ())), preferred_element_type=F32)  8.4 us
    all_to_all x1, starting transfers between devices, rows_to_owners(): lax.all_to_all(rows.reshape(devices, capacity, D + 128), ('seq', 'dp'), s...  6.29 us
    pallas_call x1, Pallas kernels, update_rows(): pl.pallas_call(update_kernel, in_specs=[hbm, hbm, vmem], out_specs=[hbm,...  5.16 us
    pallas_call x1, Pallas kernels, event_stats(): pl.pallas_call(functools.partial(stats_kernel, blk=blk, count=count), in_...  4.6 us
  transfers between devices with their start and end apart: 22, of which 8 were waited for; matrix products, arithmetic and copies ran while one was open for 15% of the time, Pallas kernels for 10%

profile of v2, /device:TPU:0, one launch (start us, length us, event | category | flops | bytes accessed | tf_op | source)
XLA Modules:
  0.0 174.3 jit_solution(12253786337553746230)
XLA Ops:
  1.5 3.1 %collective-permute-start.1 = (bf16[256,1024]{1,0:T(8,128)(2,1)}, bf16[256,1024]{1,0:T(8,128)(2,1)S(1)}, u32[]{:S(2)}, u32[]{:S(2)}) collective-permute-start(bf16[256,1024]{1,0:T(8,128)(2,1)} %param.10), channel_id=1, source_target_pairs={{0,8},{1,16},{2,10},{3,18},{4,12},{5,20},{6,14},{7,22},{8,0},{9,24... | collective-permute-start | bytes 1572872 | tf_op jit(solution)/shard_map/ppermute | solution.py:523
  9.2 1.5 constant_dynamic-slice_fusion.6
  10.8 1.6 pad_maximum_fusion.refs_4_
  14.7 16.3 %collective-permute-start.3 = (bf16[512,1024]{1,0:T(8,128)(2,1)S(1)}, bf16[512,1024]{1,0:T(8,128)(2,1)}, u32[]{:S(2)}, u32[]{:S(2)}) collective-permute-start(bf16[512,1024]{1,0:T(8,128)(2,1)S(1)} %pad_maximum_fusion.1.refs_2_), channel_id=1, source_target_pairs={{0,1},{1,0},{2,3},{3,2},{4,5},{5,4},{6,7},{7,6},{8,9},{9,8},{10,11... | collective-permute-start | bytes 3145736 | tf_op jit(solution)/shard_map/ppermute | solution.py:523
  31.7 1.7 collective-permute-start.5
  34.0 16.9 %attention_forward.1 = (bf16[1024,1024]{1,0:T(8,128)(2,1)}, bf16[1024,1024]{1,0:T(8,128)(2,1)}, bf16[1024,1024]{1,0:T(8,128)(2,1)}, f32[1024,256]{1,0:T(8,128)},...) custom-call(s32[1,3]{1,0:T(1,128)} %slice.47.refs_0_, ...), custom_call_target="tpu_custom_call" | custom-call | flops 4294967296 | bytes 12582912 | tf_op jit(solution)/shard_map/attention_forward/pallas_call | solution.py:151
  51.0 8.6 %collective-permute-start.6 = (bf16[512,1024]{1,0:T(8,128)(2,1)S(1)}, bf16[512,1024]{1,0:T(8,128)(2,1)S(1)}, u32[]{:S(2)}, u32[]{:S(2)}) collective-permute-start(bf16[512,1024]{1,0:T(8,128)(2,1)S(1)} %pad_maximum_fusion.2.refs_1_), channel_id=1, source_target_pairs={{0,1},{1,0},{2,3},{3,2},{4,5},{5,4},{6,7},{7,6},{8,9},{9,8},{10,11... | collective-permute-start | bytes 3145736 | tf_op jit(solution)/shard_map/ppermute | solution.py:523
  59.7 2.3 %collective-permute-done.6.refs_2_ = bf16[512,1024]{1,0:T(8,128)(2,1)S(1)} collective-permute-done((bf16[512,1024]{1,0:T(8,128)(2,1)S(1)}, bf16[512,1024]{1,0:T(8,128)(2,1)S(1)}, u32[]{:S(2)}, u32[]{:S(2)}) %collective-permute-start.6) | collective-permute-done | bytes 1048608 | tf_op jit(solution)/shard_map/ppermute | solution.py:523
  62.9 4.6 %event_stats.1 = (bf16[1024,1024]{1,0:T(8,128)(2,1)}, f32[1024,256]{1,0:T(8,128)}, f32[8,1024]{1,0:T(8,128)}) custom-call(s32[4]{0:T(128)} %pad_add_fusion.1.refs_1_.refs_0_, bf16[512,1024]{1,0:T(8,128)(2,1)} %copy-done.3, bf16[512,1024]{1,0:T(8,128)(2,1)} %copy-done.8, bf16[256,1024]{1,0:T(8,128)(2,1)} %constant_dynamic-slice_fusion.2.refs_3_, ...), custom_call_target="tpu_custom_call" | custom-call | flops 536870912 | bytes 6815744 | tf_op jit(solution)/shard_map/event_stats/pallas_call | solution.py:209
  67.9 1.5 collective-permute-start.9
  69.4 2.6 %collective-permute-done.8.refs_3_ = f32[8,1024]{1,0:T(8,128)S(1)} collective-permute-done((f32[8,1024]{1,0:T(8,128)}, f32[8,1024]{1,0:T(8,128)S(1)}, u32[]{:S(2)}, u32[]{:S(2)}) %collective-permute-start.8) | collective-permute-done | bytes 32800 | tf_op jit(solution)/shard_map/ppermute | solution.py:523
  72.6 16.1 %attention_backward.1 = (bf16[1024,1024]{1,0:T(8,128)(2,1)}, bf16[1024,256]{1,0:T(8,128)(2,1)}) custom-call(s32[1,3]{1,0:T(1,128)} %slice.47.refs_0_, f32[8,1024]{1,0:T(8,128)} %get-tuple-element.48.refs_1_, f32[8,1024]{1,0:T(8,128)} %copy-done.13, f32[8,1024]{1,0:T(8,128)} %copy-done.14, f32[8,1024]{1,0:T(8,128)} %copy-done.15, ...), custom_call_target="tpu_custom_call" | custom-call | flops 4294967296 | bytes 15204352 | tf_op jit(solution)/shard_map/attention_backward/pallas_call | solution.py:318
  88.7 1.8 %convolution_convert_fusion.4 = bf16[256,1024]{1,0:T(8,128)(2,1)S(1)} fusion(bf16[1024,1024]{1,0:T(8,128)(2,1)S(1)} %copy-done.5, bf16[1024,1024]{1,0:T(8,128)(2,1)} %get-tuple-element.57, s32[]{:T(128)S(6)} %select_n.201), kind=kOutput, calls=%fused_computation.12 | convolution fusion | flops 537133056 | bytes 3145732 | tf_op jit(solution)/shard_map/dot_general | solution.py:27
  90.7 1.9 %collective-permute-done.10 = bf16[256,1024]{1,0:T(8,128)(2,1)} collective-permute-done((bf16[256,1024]{1,0:T(8,128)(2,1)S(1)}, bf16[256,1024]{1,0:T(8,128)(2,1)}, u32[]{:S(2)}, u32[]{:S(2)}) %collective-permute-start.10) | collective-permute-done | bytes 524320 | tf_op jit(solution)/shard_map/ppermute | solution.py:523
  92.6 2.7 %fusion.3 = bf16[256,1024]{1,0:T(8,128)(2,1)} fusion(bf16[1024,1024]{1,0:T(8,128)(2,1)S(1)} %copy-done.5, bf16[256,1024]{1,0:T(8,128)(2,1)} %collective-permute-done.10, bf16[1024,1024]{1,0:T(8,128)(2,1)} %get-tuple-element.57, s32[]{:T(128)S(6)} %select_n.200), kind=kOutput, calls=%fused_computation.13 | convolution fusion | flops 537657344 | bytes 3670020 | tf_op jit(solution)/shard_map/dot_general | solution.py:27
  95.4 1.6 convolution_convert_fusion.3
  97.1 1.8 %collective-permute-start.20 = (bf16[256,1024]{1,0:T(8,128)(2,1)}, bf16[256,1024]{1,0:T(8,128)(2,1)}, u32[]{:S(2)}, u32[]{:S(2)}) collective-permute-start(bf16[256,1024]{1,0:T(8,128)(2,1)} %fusion.3), channel_id=1, source_target_pairs={{0,8},{1,9},{2,10},{3,11},{4,12},{5,13},{6,14},{7,15},{8,0},{9,1},... | collective-permute-start | bytes 1572872 | tf_op jit(solution)/shard_map/ppermute | solution.py:523
  98.9 2.4 %convolution_convert_fusion.1 = bf16[1024,1024]{1,0:T(8,128)(2,1)S(1)} fusion(bf16[1024,1024]{1,0:T(8,128)(2,1)S(1)} %copy-done.18, bf16[1024,1024]{1,0:T(8,128)(2,1)S(1)} %copy-done.17), kind=kOutput, calls=%fused_computation.2 | convolution fusion | flops 2148532224 | bytes 6291456 | tf_op jit(solution)/shard_map/dot_general | solution.py:454
  101.3 1.5 convolution_convert_fusion.2
  103.1 1.4 reshape.171
  109.0 1.6 collective-permute-start.11
  111.6 2.3 %fusion.4 = bf16[256,1024]{1,0:T(8,128)(2,1)S(1)} fusion(bf16[1024,1024]{1,0:T(8,128)(2,1)S(1)} %copy-done.6, bf16[256,1024]{1,0:T(8,128)(2,1)} %collective-permute-done.20, bf16[256,1024]{1,0:T(8,128)(2,1)} %collective-permute-done.19, bf16[256,1024]{1,0:T(8,128)(2,1)S(1)} %broadcast_select_fusion, bf16[1024,1024]{1,0:T(8,128)(2,1)} %get-tuple-element.57, ...), kind=kOutput, calls=%fused_computation.14 | convolution fusion | flops 538705920 | bytes 4718596 | tf_op jit(solution)/shard_map/dot_general | solution.py:27
  113.9 1.5 convolution_convert_fusion
  115.4 6.3 %all-to-all-start = ((bf16[32,16,1152]{2,1,0:T(8,128)(2,1)}), bf16[32,16,1152]{2,1,0:T(8,128)(2,1)S(1)}, u32[]{:S(2)}, u32[]{:S(2)}) async-start(bf16[32,16,1152]{2,1,0:T(8,128)(2,1)} %bitcast.28), calls=%async_computation | async-start | bytes 2359296 | tf_op jit(solution)/shard_map/all_to_all | solution.py:444
  121.7 2.0 %collective-permute-done.13 = bf16[2,256,640]{2,1,0:T(8,128)(2,1)} collective-permute-done((bf16[2,256,640]{2,1,0:T(8,128)(2,1)}, bf16[2,256,640]{2,1,0:T(8,128)(2,1)}, u32[]{:S(2)}, u32[]{:S(2)}) %collective-permute-start.13) | collective-permute-done | bytes 655392 | tf_op jit(solution)/shard_map/ppermute | solution.py:523
  125.0 3.1 %collective-permute-start.14 = (bf16[256,640]{1,0:T(8,128)(2,1)S(1)}, bf16[256,640]{1,0:T(8,128)(2,1)S(1)}, u32[]{:S(2)}, u32[]{:S(2)}) collective-permute-start(bf16[256,640]{1,0:T(8,128)(2,1)S(1)} %dynamic-slice_bitcast_fusion.3), channel_id=1, source_target_pairs={{0,2},{1,3},{2,0},{3,1},{4,6},{5,7},{6,4},{7,5},{8,10},{9,11},{10,... | collective-permute-start | bytes 983048 | tf_op jit(solution)/shard_map/ppermute | solution.py:523
  129.5 3.5 %collective-permute-start.12 = (bf16[256,640]{1,0:T(8,128)(2,1)S(1)}, bf16[256,640]{1,0:T(8,128)(2,1)S(1)}, u32[]{:S(2)}, u32[]{:S(2)}) collective-permute-start(bf16[256,640]{1,0:T(8,128)(2,1)S(1)} %dynamic-slice_bitcast_fusion.4), channel_id=1, source_target_pairs={{0,4},{1,5},{2,6},{3,7},{4,0},{5,1},{6,2},{7,3},{8,12},{9,13},{10,... | collective-permute-start | bytes 983048 | tf_op jit(solution)/shard_map/ppermute | solution.py:523
  133.0 10.8 %collective-permute-done.14 = bf16[256,640]{1,0:T(8,128)(2,1)S(1)} collective-permute-done((bf16[256,640]{1,0:T(8,128)(2,1)S(1)}, bf16[256,640]{1,0:T(8,128)(2,1)S(1)}, u32[]{:S(2)}, u32[]{:S(2)}) %collective-permute-start.14) | collective-permute-done | bytes 327712 | tf_op jit(solution)/shard_map/ppermute | solution.py:523
  144.7 3.1 %collective-permute-start.18 = (bf16[128,256]{1,0:T(8,128)(2,1)S(1)}, bf16[128,256]{1,0:T(8,128)(2,1)S(1)}, u32[]{:S(2)}, u32[]{:S(2)}) collective-permute-start(bf16[128,256]{1,0:T(8,128)(2,1)S(1)} %get-tuple-element.82), channel_id=1, source_target_pairs={{0,1},{1,3},{2,9},{3,11},{4,17},{5,19},{6,25},{7,27},{8,5},{9,7},{... | collective-permute-start | bytes 196616 | tf_op jit(solution)/shard_map/ppermute | solution.py:523
  148.7 7.4 %collective-permute-start.16 = (bf16[128,1024]{1,0:T(8,128)(2,1)S(1)}, bf16[128,1024]{1,0:T(8,128)(2,1)S(1)}, u32[]{:S(2)}, u32[]{:S(2)}) collective-permute-start(bf16[128,1024]{1,0:T(8,128)(2,1)S(1)} %get-tuple-element.78), channel_id=1, source_target_pairs={{0,1},{1,9},{2,3},{3,11},{4,5},{5,13},{6,7},{7,15},{8,17},{9,25},{... | collective-permute-start | bytes 786440 | tf_op jit(solution)/shard_map/ppermute | solution.py:523
  156.8 9.5 %collective-permute-done.16 = bf16[128,1024]{1,0:T(8,128)(2,1)S(1)} collective-permute-done((bf16[128,1024]{1,0:T(8,128)(2,1)S(1)}, bf16[128,1024]{1,0:T(8,128)(2,1)S(1)}, u32[]{:S(2)}, u32[]{:S(2)}) %collective-permute-start.16) | collective-permute-done | bytes 262176 | tf_op jit(solution)/shard_map/ppermute | solution.py:523
  168.9 5.2 %update_rows.1 = (f32[512,1024]{1,0:T(8,128)}, f32[1,512]{1,0:T(1,128)}) custom-call(bf16[512,1152]{1,0:T(8,128)(2,1)} %bitcast.62, f32[512,1024]{1,0:T(8,128)} %table_hbm.1, f32[1,512]{1,0:T(1,128)} %bitcast.75), custom_call_target="tpu_custom_call" | custom-call | flops 536870912 | bytes 5242880 | tf_op jit(solution)/shard_map/update_rows/pallas_call | solution.py:389
  (110 shorter events, 24.7 us)
Async XLA Ops:
  0.6 6.7 %copy-start = (bf16[1024,1024]{1,0:T(8,128)(2,1)S(1)}, bf16[1024,1024]{1,0:T(8,128)(2,1)}, u32[]{:S(2)}) copy-start(bf16[1024,1024]{1,0:T(8,128)(2,1)} %param.17) | copy-start | bytes 6291460
  0.6 12.8 %collective-permute-start = (bf16[256,1024]{1,0:T(8,128)(2,1)}, bf16[256,1024]{1,0:T(8,128)(2,1)S(1)}, u32[]{:S(2)}, u32[]{:S(2)}) collective-permute-start(bf16[256,1024]{1,0:T(8,128)(2,1)} %param.10), channel_id=1, source_target_pairs={{1,24},{3,26},{5,28},{7,30},{9,16},{11,18},{13,20},{15,22},{16,9},... | collective-permute-start | bytes 1572872 | tf_op jit(solution)/shard_map/ppermute | solution.py:523
  1.5 13.1 %collective-permute-start.1 = (bf16[256,1024]{1,0:T(8,128)(2,1)}, bf16[256,1024]{1,0:T(8,128)(2,1)S(1)}, u32[]{:S(2)}, u32[]{:S(2)}) collective-permute-start(bf16[256,1024]{1,0:T(8,128)(2,1)} %param.10), channel_id=1, source_target_pairs={{0,8},{1,16},{2,10},{3,18},{4,12},{5,20},{6,14},{7,22},{8,0},{9,24... | collective-permute-start | bytes 1572872 | tf_op jit(solution)/shard_map/ppermute | solution.py:523
  6.6 5.8 %collective-permute-start.2 = (s32[1,384]{1,0:T(1,128)S(1)}, s32[1,384]{1,0:T(1,128)S(1)}, u32[]{:S(2)}, u32[]{:S(2)}) collective-permute-start(s32[1,384]{1,0:T(1,128)S(1)} %pad_add_fusion), channel_id=1, source_target_pairs={{1,24},{3,26},{5,28},{7,30},{9,16},{11,18},{13,20},{15,22},{16,9},... | collective-permute-start | bytes 4616 | tf_op jit(solution)/shard_map/ppermute | solution.py:523
  10.8 3.8 %copy-start.10 = (bf16[256,1024]{1,0:T(8,128)(2,1)S(1)}, bf16[256,1024]{1,0:T(8,128)(2,1)}, u32[]{:S(2)}) copy-start(bf16[256,1024]{1,0:T(8,128)(2,1)} %param.10) | copy-start | bytes 1572868
  12.4 18.6 %copy-start.11 = (bf16[256,1024]{1,0:T(8,128)(2,1)S(1)}, bf16[256,1024]{1,0:T(8,128)(2,1)}, u32[]{:S(2)}) copy-start(bf16[256,1024]{1,0:T(8,128)(2,1)} %param.11) | copy-start | bytes 1572868
  14.7 19.3 %copy-start.9 = (bf16[512,1024]{1,0:T(8,128)(2,1)}, bf16[512,1024]{1,0:T(8,128)(2,1)S(1)}, u32[]{:S(2)}) copy-start(bf16[512,1024]{1,0:T(8,128)(2,1)S(1)} %pad_maximum_fusion.1.refs_2_) | copy-start | bytes 3145732
  14.7 19.3 %collective-permute-start.3 = (bf16[512,1024]{1,0:T(8,128)(2,1)S(1)}, bf16[512,1024]{1,0:T(8,128)(2,1)}, u32[]{:S(2)}, u32[]{:S(2)}) collective-permute-start(bf16[512,1024]{1,0:T(8,128)(2,1)S(1)} %pad_maximum_fusion.1.refs_2_), channel_id=1, source_target_pairs={{0,1},{1,0},{2,3},{3,2},{4,5},{5,4},{6,7},{7,6},{8,9},{9,8},{10,11... | collective-permute-start | bytes 3145736 | tf_op jit(solution)/shard_map/ppermute | solution.py:523
  31.0 19.9 %collective-permute-start.4 = (bf16[256,1024]{1,0:T(8,128)(2,1)S(1)}, bf16[256,1024]{1,0:T(8,128)(2,1)S(1)}, u32[]{:S(2)}, u32[]{:S(2)}) collective-permute-start(bf16[256,1024]{1,0:T(8,128)(2,1)S(1)} %copy-done.11), channel_id=1, source_target_pairs={{1,24},{3,26},{5,28},{7,30},{9,16},{11,18},{13,20},{15,22},{16,9},... | collective-permute-start | bytes 1572872 | tf_op jit(solution)/shard_map/ppermute | solution.py:523
  31.7 19.2 %collective-permute-start.5 = (bf16[256,1024]{1,0:T(8,128)(2,1)S(1)}, bf16[256,1024]{1,0:T(8,128)(2,1)S(1)}, u32[]{:S(2)}, u32[]{:S(2)}) collective-permute-start(bf16[256,1024]{1,0:T(8,128)(2,1)S(1)} %copy-done.11), channel_id=1, source_target_pairs={{0,8},{1,16},{2,10},{3,18},{4,12},{5,20},{6,14},{7,22},{8,0},{9,24... | collective-permute-start | bytes 1572872 | tf_op jit(solution)/shard_map/ppermute | solution.py:523
  51.0 10.9 %copy-start.3 = (bf16[512,1024]{1,0:T(8,128)(2,1)}, bf16[512,1024]{1,0:T(8,128)(2,1)S(1)}, u32[]{:S(2)}) copy-start(bf16[512,1024]{1,0:T(8,128)(2,1)S(1)} %pad_maximum_fusion.2.refs_1_) | copy-start | bytes 3145732
  51.0 10.9 %collective-permute-start.6 = (bf16[512,1024]{1,0:T(8,128)(2,1)S(1)}, bf16[512,1024]{1,0:T(8,128)(2,1)S(1)}, u32[]{:S(2)}, u32[]{:S(2)}) collective-permute-start(bf16[512,1024]{1,0:T(8,128)(2,1)S(1)} %pad_maximum_fusion.2.refs_1_), channel_id=1, source_target_pairs={{0,1},{1,0},{2,3},{3,2},{4,5},{5,4},{6,7},{7,6},{8,9},{9,8},{10,11... | collective-permute-start | bytes 3145736 | tf_op jit(solution)/shard_map/ppermute | solution.py:523
  67.5 1.9 %collective-permute-start.7 = (f32[8,1024]{1,0:T(8,128)}, f32[8,1024]{1,0:T(8,128)S(1)}, u32[]{:S(2)}, u32[]{:S(2)}) collective-permute-start(f32[8,1024]{1,0:T(8,128)} %get-tuple-element.48.refs_1_), channel_id=1, source_target_pairs={{0,1},{1,0},{2,3},{3,2},{4,5},{5,4},{6,7},{7,6},{8,9},{9,8},{10,11... | collective-permute-start | bytes 98312 | tf_op jit(solution)/shard_map/ppermute | solution.py:523
  67.9 4.1 %collective-permute-start.8 = (f32[8,1024]{1,0:T(8,128)}, f32[8,1024]{1,0:T(8,128)S(1)}, u32[]{:S(2)}, u32[]{:S(2)}) collective-permute-start(f32[8,1024]{1,0:T(8,128)} %get-tuple-element.48.refs_1_), channel_id=1, source_target_pairs={{0,8},{1,9},{2,10},{3,11},{4,12},{5,13},{6,14},{7,15},{8,0},{9,1},... | collective-permute-start | bytes 98312 | tf_op jit(solution)/shard_map/ppermute | solution.py:523
  67.9 4.1 %collective-permute-start.9 = (f32[8,1024]{1,0:T(8,128)}, f32[8,1024]{1,0:T(8,128)S(1)}, u32[]{:S(2)}, u32[]{:S(2)}) collective-permute-start(f32[8,1024]{1,0:T(8,128)} %get-tuple-element.48.refs_1_), channel_id=1, source_target_pairs={{0,9},{1,8},{2,11},{3,10},{4,13},{5,12},{6,15},{7,14},{8,1},{9,0},... | collective-permute-start | bytes 98312 | tf_op jit(solution)/shard_map/ppermute | solution.py:523
  72.6 16.1 %copy-start.5 = (bf16[1024,1024]{1,0:T(8,128)(2,1)S(1)}, bf16[1024,1024]{1,0:T(8,128)(2,1)}, u32[]{:S(2)}) copy-start(bf16[1024,1024]{1,0:T(8,128)(2,1)} %pad_maximum_fusion.refs_4_) | copy-start | bytes 6291460
  90.5 2.1 %collective-permute-start.10 = (bf16[256,1024]{1,0:T(8,128)(2,1)S(1)}, bf16[256,1024]{1,0:T(8,128)(2,1)}, u32[]{:S(2)}, u32[]{:S(2)}) collective-permute-start(bf16[256,1024]{1,0:T(8,128)(2,1)S(1)} %convolution_convert_fusion.4), channel_id=1, source_target_pairs={{0,1},{1,0},{2,3},{3,2},{4,5},{5,4},{6,7},{7,6},{8,9},{9,8},{10,11... | collective-permute-start | bytes 1572872 | tf_op jit(solution)/shard_map/ppermute | solution.py:523
  90.7 4.6 %copy-start.17 = (bf16[1024,1024]{1,0:T(8,128)(2,1)S(1)}, bf16[1024,1024]{1,0:T(8,128)(2,1)}, u32[]{:S(2)}) copy-start(bf16[1024,1024]{1,0:T(8,128)(2,1)} %get-tuple-element.57) | copy-start | bytes 6291460
  97.0 13.6 %collective-permute-start.19 = (bf16[256,1024]{1,0:T(8,128)(2,1)}, bf16[256,1024]{1,0:T(8,128)(2,1)}, u32[]{:S(2)}, u32[]{:S(2)}) collective-permute-start(bf16[256,1024]{1,0:T(8,128)(2,1)} %convolution_convert_fusion.3), channel_id=1, source_target_pairs={{0,1},{1,0},{2,3},{3,2},{4,5},{5,4},{6,7},{7,6},{8,9},{9,8},{10,11... | collective-permute-start | bytes 1572872 | tf_op jit(solution)/shard_map/ppermute | solution.py:523
  97.1 14.5 %collective-permute-start.20 = (bf16[256,1024]{1,0:T(8,128)(2,1)}, bf16[256,1024]{1,0:T(8,128)(2,1)}, u32[]{:S(2)}, u32[]{:S(2)}) collective-permute-start(bf16[256,1024]{1,0:T(8,128)(2,1)} %fusion.3), channel_id=1, source_target_pairs={{0,8},{1,9},{2,10},{3,11},{4,12},{5,13},{6,14},{7,15},{8,0},{9,1},... | collective-permute-start | bytes 1572872 | tf_op jit(solution)/shard_map/ppermute | solution.py:523
  104.9 6.7 %copy-start.6 = (bf16[1024,1024]{1,0:T(8,128)(2,1)S(1)}, bf16[1024,1024]{1,0:T(8,128)(2,1)}, u32[]{:S(2)}) copy-start(bf16[1024,1024]{1,0:T(8,128)(2,1)} %pad_maximum_fusion.refs_4_) | copy-start | bytes 6291460
  106.7 17.0 %collective-permute-start.13 = (bf16[2,256,640]{2,1,0:T(8,128)(2,1)}, bf16[2,256,640]{2,1,0:T(8,128)(2,1)}, u32[]{:S(2)}, u32[]{:S(2)}) collective-permute-start(bf16[2,256,640]{2,1,0:T(8,128)(2,1)} %pad_maximum_fusion.3), channel_id=1, source_target_pairs={{0,4},{1,5},{2,6},{3,7},{4,0},{5,1},{6,2},{7,3},{8,12},{9,13},{10,... | collective-permute-start | bytes 1966088 | tf_op jit(solution)/shard_map/ppermute | solution.py:523
  109.0 19.1 %collective-permute-start.11 = (bf16[2,256,640]{2,1,0:T(8,128)(2,1)}, bf16[2,256,640]{2,1,0:T(8,128)(2,1)}, u32[]{:S(2)}, u32[]{:S(2)}) collective-permute-start(bf16[2,256,640]{2,1,0:T(8,128)(2,1)} %dynamic-slice_bitcast_fusion), channel_id=1, source_target_pairs={{0,2},{1,3},{2,0},{3,1},{4,6},{5,7},{6,4},{7,5},{8,10},{9,11},{10,... | collective-permute-start | bytes 1966088 | tf_op jit(solution)/shard_map/ppermute | solution.py:523
  113.9 9.8 %copy-start.7 = (bf16[2,256,384]{2,1,0:T(8,128)(2,1)S(1)}, bf16[2,256,384]{2,1,0:T(8,128)(2,1)}, u32[]{:S(2)}) copy-start(bf16[2,256,384]{2,1,0:T(8,128)(2,1)} %get-tuple-element.71) | copy-start | bytes 1179652
  115.4 52.4 %all-to-all-start = ((bf16[32,16,1152]{2,1,0:T(8,128)(2,1)}), bf16[32,16,1152]{2,1,0:T(8,128)(2,1)S(1)}, u32[]{:S(2)}, u32[]{:S(2)}) async-start(bf16[32,16,1152]{2,1,0:T(8,128)(2,1)} %bitcast.28), calls=%async_computation | async-start | bytes 2359296 | tf_op jit(solution)/shard_map/all_to_all | solution.py:444
  125.0 18.8 %collective-permute-start.14 = (bf16[256,640]{1,0:T(8,128)(2,1)S(1)}, bf16[256,640]{1,0:T(8,128)(2,1)S(1)}, u32[]{:S(2)}, u32[]{:S(2)}) collective-permute-start(bf16[256,640]{1,0:T(8,128)(2,1)S(1)} %dynamic-slice_bitcast_fusion.3), channel_id=1, source_target_pairs={{0,2},{1,3},{2,0},{3,1},{4,6},{5,7},{6,4},{7,5},{8,10},{9,11},{10,... | collective-permute-start | bytes 983048 | tf_op jit(solution)/shard_map/ppermute | solution.py:523
  129.5 18.3 %collective-permute-start.12 = (bf16[256,640]{1,0:T(8,128)(2,1)S(1)}, bf16[256,640]{1,0:T(8,128)(2,1)S(1)}, u32[]{:S(2)}, u32[]{:S(2)}) collective-permute-start(bf16[256,640]{1,0:T(8,128)(2,1)S(1)} %dynamic-slice_bitcast_fusion.4), channel_id=1, source_target_pairs={{0,4},{1,5},{2,6},{3,7},{4,0},{5,1},{6,2},{7,3},{8,12},{9,13},{10,... | collective-permute-start | bytes 983048 | tf_op jit(solution)/shard_map/ppermute | solution.py:523
  144.0 12.1 %collective-permute-start.17 = (bf16[128,256]{1,0:T(8,128)(2,1)S(1)}, bf16[128,256]{1,0:T(8,128)(2,1)S(1)}, u32[]{:S(2)}, u32[]{:S(2)}) collective-permute-start(bf16[128,256]{1,0:T(8,128)(2,1)S(1)} %get-tuple-element.81), channel_id=1, source_target_pairs={{0,0},{1,2},{2,8},{3,10},{4,16},{5,18},{6,24},{7,26},{8,4},{9,6},{... | collective-permute-start | bytes 196616 | tf_op jit(solution)/shard_map/ppermute | solution.py:523
  144.7 11.4 %collective-permute-start.18 = (bf16[128,256]{1,0:T(8,128)(2,1)S(1)}, bf16[128,256]{1,0:T(8,128)(2,1)S(1)}, u32[]{:S(2)}, u32[]{:S(2)}) collective-permute-start(bf16[128,256]{1,0:T(8,128)(2,1)S(1)} %get-tuple-element.82), channel_id=1, source_target_pairs={{0,1},{1,3},{2,9},{3,11},{4,17},{5,19},{6,25},{7,27},{8,5},{9,7},{... | collective-permute-start | bytes 196616 | tf_op jit(solution)/shard_map/ppermute | solution.py:523
  148.0 8.8 %collective-permute-start.15 = (bf16[128,1024]{1,0:T(8,128)(2,1)S(1)}, bf16[128,1024]{1,0:T(8,128)(2,1)S(1)}, u32[]{:S(2)}, u32[]{:S(2)}) collective-permute-start(bf16[128,1024]{1,0:T(8,128)(2,1)S(1)} %get-tuple-element.77), channel_id=1, source_target_pairs={{0,0},{1,8},{2,2},{3,10},{4,4},{5,12},{6,6},{7,14},{8,16},{9,24},{... | collective-permute-start | bytes 786440 | tf_op jit(solution)/shard_map/ppermute | solution.py:523
  148.7 17.6 %collective-permute-start.16 = (bf16[128,1024]{1,0:T(8,128)(2,1)S(1)}, bf16[128,1024]{1,0:T(8,128)(2,1)S(1)}, u32[]{:S(2)}, u32[]{:S(2)}) collective-permute-start(bf16[128,1024]{1,0:T(8,128)(2,1)S(1)} %get-tuple-element.78), channel_id=1, source_target_pairs={{0,1},{1,9},{2,3},{3,11},{4,5},{5,13},{6,7},{7,15},{8,17},{9,25},{... | collective-permute-start | bytes 786440 | tf_op jit(solution)/shard_map/ppermute | solution.py:523
  167.0 7.1 %copy-start.1 = (bf16[1024,1024]{1,0:T(8,128)(2,1)S(1)}, bf16[1024,1024]{1,0:T(8,128)(2,1)}, u32[]{:S(2)}) copy-start(bf16[1024,1024]{1,0:T(8,128)(2,1)} %param.17) | copy-start | bytes 6291460
  (9 other events, 16.0 us)

commit v3 on v0

--- a/solution.py
+++ b/solution.py
@@ -373,7 +373,7 @@
 def update_rows(got_rows, emb_table, row_accum):
     rows_own = emb_table.shape[0]
     slots = got_rows.shape[0]
-    blk = min(256, rows_own)
+    blk = min(512, rows_own)
     new_table, new_accum = pl.pallas_call(
         update_kernel,
         grid=(rows_own // blk,),

time: 173 us -> 174 us (level)
  starting transfers between devices: 59.9 us -> 54.2 us
  Pallas kernels: 41.5 us -> 44.9 us
  waiting for transfers between devices: 34.7 us -> 36.5 us
    ppermute x21, starting transfers between devices: 54.4 us -> 50.1 us  [send(): return lax.ppermute(array, ('seq', 'dp'), steps)]
    ppermute x21, waiting for transfers between devices: 34.7 us -> 36.5 us  [send(): return lax.ppermute(array, ('seq', 'dp'), steps)]
  transfers between devices with their start and end apart: 22 -> 22, of which waited for: 9 -> 9; matrix products, arithmetic and copies ran while one was open for 15% -> 15% of each run, Pallas kernels for 10% -> 11%
where the time goes in v3:
time: 174 us; the launch traced here: 172 us
  starting transfers between devices  54.2 us (31%)
  Pallas kernels  44.9 us (26%)
  waiting for transfers between devices  36.5 us (21%)
  matrix products  14.1 us (8%)
  local copies, waits for them, and re-layouts  10.8 us (6%)
  other arithmetic  10.6 us (6%)
    ppermute x21, starting transfers between devices, send(): return lax.ppermute(array, ('seq', 'dp'), steps)  50.1 us
    ppermute x21, waiting for transfers between devices, send(): return lax.ppermute(array, ('seq', 'dp'), steps)  36.5 us
    pallas_call x1, Pallas kernels, forward_attention(): pl.pallas_call(functools.partial(forward_kernel, blk=blk, users=users, ma...  18.1 us
    pallas_call x1, Pallas kernels, backward_attention(): pl.pallas_call(functools.partial(backward_kernel, blk=blk, users=users, m...  17.3 us
    dot_general x4, matrix products, dot_nt(): lax.dot_general(a, b, (((1,), (1,)), ((), ())), preferred_element_type=F32)  8.4 us
    pallas_call x1, Pallas kernels, update_rows(): pl.pallas_call(update_kernel, grid=(rows_own // blk,), in_specs=[pl.Block...  4.78 us
    pallas_call x1, Pallas kernels, event_stats(): pl.pallas_call(functools.partial(stats_kernel, blk=blk, count=count), in_...  4.6 us
    all_to_all x1, starting transfers between devices, rows_to_owners(): lax.all_to_all(rows.reshape(devices, capacity, D + 128), ('seq', 'dp'), s...  4.09 us
  transfers between devices with their start and end apart: 22, of which 9 were waited for; matrix products, arithmetic and copies ran while one was open for 15% of the time, Pallas kernels for 11%

profile of v3, /device:TPU:0, one launch (start us, length us, event | category | flops | bytes accessed | tf_op | source)
XLA Modules:
  0.0 172.1 jit_solution(16059239839536354346)
XLA Ops:
  1.5 3.1 %collective-permute-start.1 = (bf16[256,1024]{1,0:T(8,128)(2,1)}, bf16[256,1024]{1,0:T(8,128)(2,1)S(1)}, u32[]{:S(2)}, u32[]{:S(2)}) collective-permute-start(bf16[256,1024]{1,0:T(8,128)(2,1)} %param.10), channel_id=1, source_target_pairs={{0,8},{1,16},{2,10},{3,18},{4,12},{5,20},{6,14},{7,22},{8,0},{9,24... | collective-permute-start | bytes 1572872 | tf_op jit(solution)/shard_map/ppermute | solution.py:514
  9.2 1.5 constant_dynamic-slice_fusion.6
  10.8 1.6 pad_maximum_fusion.refs_4_
  14.7 16.3 %collective-permute-start.3 = (bf16[512,1024]{1,0:T(8,128)(2,1)S(1)}, bf16[512,1024]{1,0:T(8,128)(2,1)}, u32[]{:S(2)}, u32[]{:S(2)}) collective-permute-start(bf16[512,1024]{1,0:T(8,128)(2,1)S(1)} %pad_maximum_fusion.1.refs_2_), channel_id=1, source_target_pairs={{0,1},{1,0},{2,3},{3,2},{4,5},{5,4},{6,7},{7,6},{8,9},{9,8},{10,11... | collective-permute-start | bytes 3145736 | tf_op jit(solution)/shard_map/ppermute | solution.py:514
  31.7 1.7 collective-permute-start.5
  34.0 18.1 %attention_forward.1 = (bf16[1024,1024]{1,0:T(8,128)(2,1)}, bf16[1024,1024]{1,0:T(8,128)(2,1)}, bf16[1024,1024]{1,0:T(8,128)(2,1)}, f32[1024,256]{1,0:T(8,128)},...) custom-call(s32[1,3]{1,0:T(1,128)} %slice.47.refs_0_, ...), custom_call_target="tpu_custom_call" | custom-call | flops 4294967296 | bytes 12582912 | tf_op jit(solution)/shard_map/attention_forward/pallas_call | solution.py:151
  52.3 7.4 %collective-permute-start.6 = (bf16[512,1024]{1,0:T(8,128)(2,1)S(1)}, bf16[512,1024]{1,0:T(8,128)(2,1)S(1)}, u32[]{:S(2)}, u32[]{:S(2)}) collective-permute-start(bf16[512,1024]{1,0:T(8,128)(2,1)S(1)} %pad_maximum_fusion.2.refs_1_), channel_id=1, source_target_pairs={{0,1},{1,0},{2,3},{3,2},{4,5},{5,4},{6,7},{7,6},{8,9},{9,8},{10,11... | collective-permute-start | bytes 3145736 | tf_op jit(solution)/shard_map/ppermute | solution.py:514
  59.7 2.3 %collective-permute-done.6.refs_2_ = bf16[512,1024]{1,0:T(8,128)(2,1)S(1)} collective-permute-done((bf16[512,1024]{1,0:T(8,128)(2,1)S(1)}, bf16[512,1024]{1,0:T(8,128)(2,1)S(1)}, u32[]{:S(2)}, u32[]{:S(2)}) %collective-permute-start.6) | collective-permute-done | bytes 1048608 | tf_op jit(solution)/shard_map/ppermute | solution.py:514
  62.9 4.6 %event_stats.1 = (bf16[1024,1024]{1,0:T(8,128)(2,1)}, f32[1024,256]{1,0:T(8,128)}, f32[8,1024]{1,0:T(8,128)}) custom-call(s32[4]{0:T(128)} %pad_add_fusion.1.refs_1_.refs_0_, bf16[512,1024]{1,0:T(8,128)(2,1)} %copy-done.3, bf16[512,1024]{1,0:T(8,128)(2,1)} %copy-done.8, bf16[256,1024]{1,0:T(8,128)(2,1)} %constant_dynamic-slice_fusion.2.refs_3_, ...), custom_call_target="tpu_custom_call" | custom-call | flops 536870912 | bytes 6815744 | tf_op jit(solution)/shard_map/event_stats/pallas_call | solution.py:209
  67.9 1.5 collective-permute-start.9
  69.4 2.6 %collective-permute-done.8.refs_3_ = f32[8,1024]{1,0:T(8,128)S(1)} collective-permute-done((f32[8,1024]{1,0:T(8,128)}, f32[8,1024]{1,0:T(8,128)S(1)}, u32[]{:S(2)}, u32[]{:S(2)}) %collective-permute-start.8) | collective-permute-done | bytes 32800 | tf_op jit(solution)/shard_map/ppermute | solution.py:514
  72.6 17.3 %attention_backward.1 = (bf16[1024,1024]{1,0:T(8,128)(2,1)}, bf16[1024,256]{1,0:T(8,128)(2,1)}) custom-call(s32[1,3]{1,0:T(1,128)} %slice.47.refs_0_, f32[8,1024]{1,0:T(8,128)} %get-tuple-element.48.refs_1_, f32[8,1024]{1,0:T(8,128)} %copy-done.13, f32[8,1024]{1,0:T(8,128)} %copy-done.14, f32[8,1024]{1,0:T(8,128)} %copy-done.15, ...), custom_call_target="tpu_custom_call" | custom-call | flops 4294967296 | bytes 15204352 | tf_op jit(solution)/shard_map/attention_backward/pallas_call | solution.py:318
  90.0 1.8 %convolution_convert_fusion.4 = bf16[256,1024]{1,0:T(8,128)(2,1)S(1)} fusion(bf16[1024,1024]{1,0:T(8,128)(2,1)S(1)} %copy-done.5, bf16[1024,1024]{1,0:T(8,128)(2,1)} %get-tuple-element.57, s32[]{:T(128)S(6)} %select_n.201), kind=kOutput, calls=%fused_computation.12 | convolution fusion | flops 537133056 | bytes 3145732 | tf_op jit(solution)/shard_map/dot_general | solution.py:27
  92.0 1.9 %collective-permute-done.10 = bf16[256,1024]{1,0:T(8,128)(2,1)} collective-permute-done((bf16[256,1024]{1,0:T(8,128)(2,1)S(1)}, bf16[256,1024]{1,0:T(8,128)(2,1)}, u32[]{:S(2)}, u32[]{:S(2)}) %collective-permute-start.10) | collective-permute-done | bytes 524320 | tf_op jit(solution)/shard_map/ppermute | solution.py:514
  93.9 2.7 %fusion.3 = bf16[256,1024]{1,0:T(8,128)(2,1)} fusion(bf16[1024,1024]{1,0:T(8,128)(2,1)S(1)} %copy-done.5, bf16[256,1024]{1,0:T(8,128)(2,1)} %collective-permute-done.10, bf16[1024,1024]{1,0:T(8,128)(2,1)} %get-tuple-element.57, s32[]{:T(128)S(6)} %select_n.200), kind=kOutput, calls=%fused_computation.13 | convolution fusion | flops 537657344 | bytes 3670020 | tf_op jit(solution)/shard_map/dot_general | solution.py:27
  96.7 1.6 convolution_convert_fusion.3
  98.4 1.7 %collective-permute-start.20 = (bf16[256,1024]{1,0:T(8,128)(2,1)}, bf16[256,1024]{1,0:T(8,128)(2,1)}, u32[]{:S(2)}, u32[]{:S(2)}) collective-permute-start(bf16[256,1024]{1,0:T(8,128)(2,1)} %fusion.3), channel_id=1, source_target_pairs={{0,8},{1,9},{2,10},{3,11},{4,12},{5,13},{6,14},{7,15},{8,0},{9,1},... | collective-permute-start | bytes 1572872 | tf_op jit(solution)/shard_map/ppermute | solution.py:514
  100.2 2.4 %convolution_convert_fusion.1 = bf16[1024,1024]{1,0:T(8,128)(2,1)S(1)} fusion(bf16[1024,1024]{1,0:T(8,128)(2,1)S(1)} %copy-done.18, bf16[1024,1024]{1,0:T(8,128)(2,1)S(1)} %copy-done.17), kind=kOutput, calls=%fused_computation.2 | convolution fusion | flops 2148532224 | bytes 6291456 | tf_op jit(solution)/shard_map/dot_general | solution.py:445
  102.6 1.5 convolution_convert_fusion.2
  104.4 1.4 reshape.171
  109.0 1.7 collective-permute-start.11
  110.7 2.2 %collective-permute-done.20 = bf16[256,1024]{1,0:T(8,128)(2,1)} collective-permute-done((bf16[256,1024]{1,0:T(8,128)(2,1)}, bf16[256,1024]{1,0:T(8,128)(2,1)}, u32[]{:S(2)}, u32[]{:S(2)}) %collective-permute-start.20) | collective-permute-done | bytes 524320 | tf_op jit(solution)/shard_map/ppermute | solution.py:514
  112.9 2.3 %fusion.4 = bf16[256,1024]{1,0:T(8,128)(2,1)S(1)} fusion(bf16[1024,1024]{1,0:T(8,128)(2,1)S(1)} %copy-done.6, bf16[256,1024]{1,0:T(8,128)(2,1)} %collective-permute-done.20, bf16[256,1024]{1,0:T(8,128)(2,1)} %collective-permute-done.19, bf16[256,1024]{1,0:T(8,128)(2,1)S(1)} %broadcast_select_fusion, bf16[1024,1024]{1,0:T(8,128)(2,1)} %get-tuple-element.57, ...), kind=kOutput, calls=%fused_computation.14 | convolution fusion | flops 538705920 | bytes 4718596 | tf_op jit(solution)/shard_map/dot_general | solution.py:27
  115.2 1.5 convolution_convert_fusion
  116.7 4.1 %all-to-all-start = ((bf16[32,16,1152]{2,1,0:T(8,128)(2,1)}), bf16[32,16,1152]{2,1,0:T(8,128)(2,1)S(1)}, u32[]{:S(2)}, u32[]{:S(2)}) async-start(bf16[32,16,1152]{2,1,0:T(8,128)(2,1)} %bitcast.28), calls=%async_computation | async-start | bytes 2359296 | tf_op jit(solution)/shard_map/all_to_all | solution.py:435
  120.8 5.8 %collective-permute-done.13 = bf16[2,256,640]{2,1,0:T(8,128)(2,1)} collective-permute-done((bf16[2,256,640]{2,1,0:T(8,128)(2,1)}, bf16[2,256,640]{2,1,0:T(8,128)(2,1)}, u32[]{:S(2)}, u32[]{:S(2)}) %collective-permute-start.13) | collective-permute-done | bytes 655392 | tf_op jit(solution)/shard_map/ppermute | solution.py:514
  131.6 2.2 %collective-permute-start.12 = (bf16[256,640]{1,0:T(8,128)(2,1)S(1)}, bf16[256,640]{1,0:T(8,128)(2,1)S(1)}, u32[]{:S(2)}, u32[]{:S(2)}) collective-permute-start(bf16[256,640]{1,0:T(8,128)(2,1)S(1)} %dynamic-slice_bitcast_fusion.4), channel_id=1, source_target_pairs={{0,4},{1,5},{2,6},{3,7},{4,0},{5,1},{6,2},{7,3},{8,12},{9,13},{10,... | collective-permute-start | bytes 983048 | tf_op jit(solution)/shard_map/ppermute | solution.py:514
  133.8 10.2 %collective-permute-done.14 = bf16[256,640]{1,0:T(8,128)(2,1)S(1)} collective-permute-done((bf16[256,640]{1,0:T(8,128)(2,1)S(1)}, bf16[256,640]{1,0:T(8,128)(2,1)S(1)}, u32[]{:S(2)}, u32[]{:S(2)}) %collective-permute-start.14) | collective-permute-done | bytes 327712 | tf_op jit(solution)/shard_map/ppermute | solution.py:514
  144.8 2.9 %collective-permute-start.18 = (bf16[128,256]{1,0:T(8,128)(2,1)S(1)}, bf16[128,256]{1,0:T(8,128)(2,1)S(1)}, u32[]{:S(2)}, u32[]{:S(2)}) collective-permute-start(bf16[128,256]{1,0:T(8,128)(2,1)S(1)} %get-tuple-element.82), channel_id=1, source_target_pairs={{0,1},{1,3},{2,9},{3,11},{4,17},{5,19},{6,25},{7,27},{8,5},{9,7},{... | collective-permute-start | bytes 196616 | tf_op jit(solution)/shard_map/ppermute | solution.py:514
  148.6 6.2 %collective-permute-start.16 = (bf16[128,1024]{1,0:T(8,128)(2,1)S(1)}, bf16[128,1024]{1,0:T(8,128)(2,1)S(1)}, u32[]{:S(2)}, u32[]{:S(2)}) collective-permute-start(bf16[128,1024]{1,0:T(8,128)(2,1)S(1)} %get-tuple-element.78), channel_id=1, source_target_pairs={{0,1},{1,9},{2,3},{3,11},{4,5},{5,13},{6,7},{7,15},{8,17},{9,25},{... | collective-permute-start | bytes 786440 | tf_op jit(solution)/shard_map/ppermute | solution.py:514
  155.5 9.2 %collective-permute-done.16 = bf16[128,1024]{1,0:T(8,128)(2,1)S(1)} collective-permute-done((bf16[128,1024]{1,0:T(8,128)(2,1)S(1)}, bf16[128,1024]{1,0:T(8,128)(2,1)S(1)}, u32[]{:S(2)}, u32[]{:S(2)}) %collective-permute-start.16) | collective-permute-done | bytes 262176 | tf_op jit(solution)/shard_map/ppermute | solution.py:514
  167.3 4.8 %update_rows.1 = (f32[512,1024]{1,0:T(8,128)}, f32[1,512]{1,0:T(1,128)}) custom-call(bf16[512,1152]{1,0:T(8,128)(2,1)} %bitcast.62, f32[512,1024]{1,0:T(8,128)} %table_ref.1, f32[1,512]{1,0:T(1,128)} %bitcast.75), custom_call_target="tpu_custom_call" | custom-call | flops 536870912 | bytes 5242880 | tf_op jit(solution)/shard_map/update_rows/pallas_call | solution.py:377
  (110 shorter events, 24.8 us)
Async XLA Ops:
  0.6 6.7 %copy-start = (bf16[1024,1024]{1,0:T(8,128)(2,1)S(1)}, bf16[1024,1024]{1,0:T(8,128)(2,1)}, u32[]{:S(2)}) copy-start(bf16[1024,1024]{1,0:T(8,128)(2,1)} %param.17) | copy-start | bytes 6291460
  0.6 12.8 %collective-permute-start = (bf16[256,1024]{1,0:T(8,128)(2,1)}, bf16[256,1024]{1,0:T(8,128)(2,1)S(1)}, u32[]{:S(2)}, u32[]{:S(2)}) collective-permute-start(bf16[256,1024]{1,0:T(8,128)(2,1)} %param.10), channel_id=1, source_target_pairs={{1,24},{3,26},{5,28},{7,30},{9,16},{11,18},{13,20},{15,22},{16,9},... | collective-permute-start | bytes 1572872 | tf_op jit(solution)/shard_map/ppermute | solution.py:514
  1.5 13.1 %collective-permute-start.1 = (bf16[256,1024]{1,0:T(8,128)(2,1)}, bf16[256,1024]{1,0:T(8,128)(2,1)S(1)}, u32[]{:S(2)}, u32[]{:S(2)}) collective-permute-start(bf16[256,1024]{1,0:T(8,128)(2,1)} %param.10), channel_id=1, source_target_pairs={{0,8},{1,16},{2,10},{3,18},{4,12},{5,20},{6,14},{7,22},{8,0},{9,24... | collective-permute-start | bytes 1572872 | tf_op jit(solution)/shard_map/ppermute | solution.py:514
  6.6 5.8 %collective-permute-start.2 = (s32[1,384]{1,0:T(1,128)S(1)}, s32[1,384]{1,0:T(1,128)S(1)}, u32[]{:S(2)}, u32[]{:S(2)}) collective-permute-start(s32[1,384]{1,0:T(1,128)S(1)} %pad_add_fusion), channel_id=1, source_target_pairs={{1,24},{3,26},{5,28},{7,30},{9,16},{11,18},{13,20},{15,22},{16,9},... | collective-permute-start | bytes 4616 | tf_op jit(solution)/shard_map/ppermute | solution.py:514
  10.8 3.8 %copy-start.10 = (bf16[256,1024]{1,0:T(8,128)(2,1)S(1)}, bf16[256,1024]{1,0:T(8,128)(2,1)}, u32[]{:S(2)}) copy-start(bf16[256,1024]{1,0:T(8,128)(2,1)} %param.10) | copy-start | bytes 1572868
  12.4 18.6 %copy-start.11 = (bf16[256,1024]{1,0:T(8,128)(2,1)S(1)}, bf16[256,1024]{1,0:T(8,128)(2,1)}, u32[]{:S(2)}) copy-start(bf16[256,1024]{1,0:T(8,128)(2,1)} %param.11) | copy-start | bytes 1572868
  14.7 19.3 %copy-start.9 = (bf16[512,1024]{1,0:T(8,128)(2,1)}, bf16[512,1024]{1,0:T(8,128)(2,1)S(1)}, u32[]{:S(2)}) copy-start(bf16[512,1024]{1,0:T(8,128)(2,1)S(1)} %pad_maximum_fusion.1.refs_2_) | copy-start | bytes 3145732
  14.7 19.3 %collective-permute-start.3 = (bf16[512,1024]{1,0:T(8,128)(2,1)S(1)}, bf16[512,1024]{1,0:T(8,128)(2,1)}, u32[]{:S(2)}, u32[]{:S(2)}) collective-permute-start(bf16[512,1024]{1,0:T(8,128)(2,1)S(1)} %pad_maximum_fusion.1.refs_2_), channel_id=1, source_target_pairs={{0,1},{1,0},{2,3},{3,2},{4,5},{5,4},{6,7},{7,6},{8,9},{9,8},{10,11... | collective-permute-start | bytes 3145736 | tf_op jit(solution)/shard_map/ppermute | solution.py:514
  31.0 21.1 %collective-permute-start.4 = (bf16[256,1024]{1,0:T(8,128)(2,1)S(1)}, bf16[256,1024]{1,0:T(8,128)(2,1)S(1)}, u32[]{:S(2)}, u32[]{:S(2)}) collective-permute-start(bf16[256,1024]{1,0:T(8,128)(2,1)S(1)} %copy-done.11), channel_id=1, source_target_pairs={{1,24},{3,26},{5,28},{7,30},{9,16},{11,18},{13,20},{15,22},{16,9},... | collective-permute-start | bytes 1572872 | tf_op jit(solution)/shard_map/ppermute | solution.py:514
  31.7 20.5 %collective-permute-start.5 = (bf16[256,1024]{1,0:T(8,128)(2,1)S(1)}, bf16[256,1024]{1,0:T(8,128)(2,1)S(1)}, u32[]{:S(2)}, u32[]{:S(2)}) collective-permute-start(bf16[256,1024]{1,0:T(8,128)(2,1)S(1)} %copy-done.11), channel_id=1, source_target_pairs={{0,8},{1,16},{2,10},{3,18},{4,12},{5,20},{6,14},{7,22},{8,0},{9,24... | collective-permute-start | bytes 1572872 | tf_op jit(solution)/shard_map/ppermute | solution.py:514
  52.3 9.7 %copy-start.3 = (bf16[512,1024]{1,0:T(8,128)(2,1)}, bf16[512,1024]{1,0:T(8,128)(2,1)S(1)}, u32[]{:S(2)}) copy-start(bf16[512,1024]{1,0:T(8,128)(2,1)S(1)} %pad_maximum_fusion.2.refs_1_) | copy-start | bytes 3145732
  52.3 9.6 %collective-permute-start.6 = (bf16[512,1024]{1,0:T(8,128)(2,1)S(1)}, bf16[512,1024]{1,0:T(8,128)(2,1)S(1)}, u32[]{:S(2)}, u32[]{:S(2)}) collective-permute-start(bf16[512,1024]{1,0:T(8,128)(2,1)S(1)} %pad_maximum_fusion.2.refs_1_), channel_id=1, source_target_pairs={{0,1},{1,0},{2,3},{3,2},{4,5},{5,4},{6,7},{7,6},{8,9},{9,8},{10,11... | collective-permute-start | bytes 3145736 | tf_op jit(solution)/shard_map/ppermute | solution.py:514
  67.5 1.9 %collective-permute-start.7 = (f32[8,1024]{1,0:T(8,128)}, f32[8,1024]{1,0:T(8,128)S(1)}, u32[]{:S(2)}, u32[]{:S(2)}) collective-permute-start(f32[8,1024]{1,0:T(8,128)} %get-tuple-element.48.refs_1_), channel_id=1, source_target_pairs={{0,1},{1,0},{2,3},{3,2},{4,5},{5,4},{6,7},{7,6},{8,9},{9,8},{10,11... | collective-permute-start | bytes 98312 | tf_op jit(solution)/shard_map/ppermute | solution.py:514
  67.9 4.1 %collective-permute-start.8 = (f32[8,1024]{1,0:T(8,128)}, f32[8,1024]{1,0:T(8,128)S(1)}, u32[]{:S(2)}, u32[]{:S(2)}) collective-permute-start(f32[8,1024]{1,0:T(8,128)} %get-tuple-element.48.refs_1_), channel_id=1, source_target_pairs={{0,8},{1,9},{2,10},{3,11},{4,12},{5,13},{6,14},{7,15},{8,0},{9,1},... | collective-permute-start | bytes 98312 | tf_op jit(solution)/shard_map/ppermute | solution.py:514
  67.9 4.1 %collective-permute-start.9 = (f32[8,1024]{1,0:T(8,128)}, f32[8,1024]{1,0:T(8,128)S(1)}, u32[]{:S(2)}, u32[]{:S(2)}) collective-permute-start(f32[8,1024]{1,0:T(8,128)} %get-tuple-element.48.refs_1_), channel_id=1, source_target_pairs={{0,9},{1,8},{2,11},{3,10},{4,13},{5,12},{6,15},{7,14},{8,1},{9,0},... | collective-permute-start | bytes 98312 | tf_op jit(solution)/shard_map/ppermute | solution.py:514
  72.6 17.3 %copy-start.5 = (bf16[1024,1024]{1,0:T(8,128)(2,1)S(1)}, bf16[1024,1024]{1,0:T(8,128)(2,1)}, u32[]{:S(2)}) copy-start(bf16[1024,1024]{1,0:T(8,128)(2,1)} %pad_maximum_fusion.refs_4_) | copy-start | bytes 6291460
  91.8 2.1 %collective-permute-start.10 = (bf16[256,1024]{1,0:T(8,128)(2,1)S(1)}, bf16[256,1024]{1,0:T(8,128)(2,1)}, u32[]{:S(2)}, u32[]{:S(2)}) collective-permute-start(bf16[256,1024]{1,0:T(8,128)(2,1)S(1)} %convolution_convert_fusion.4), channel_id=1, source_target_pairs={{0,1},{1,0},{2,3},{3,2},{4,5},{5,4},{6,7},{7,6},{8,9},{9,8},{10,11... | collective-permute-start | bytes 1572872 | tf_op jit(solution)/shard_map/ppermute | solution.py:514
  92.0 4.6 %copy-start.17 = (bf16[1024,1024]{1,0:T(8,128)(2,1)S(1)}, bf16[1024,1024]{1,0:T(8,128)(2,1)}, u32[]{:S(2)}) copy-start(bf16[1024,1024]{1,0:T(8,128)(2,1)} %get-tuple-element.57) | copy-start | bytes 6291460
  98.2 12.5 %collective-permute-start.19 = (bf16[256,1024]{1,0:T(8,128)(2,1)}, bf16[256,1024]{1,0:T(8,128)(2,1)}, u32[]{:S(2)}, u32[]{:S(2)}) collective-permute-start(bf16[256,1024]{1,0:T(8,128)(2,1)} %convolution_convert_fusion.3), channel_id=1, source_target_pairs={{0,1},{1,0},{2,3},{3,2},{4,5},{5,4},{6,7},{7,6},{8,9},{9,8},{10,11... | collective-permute-start | bytes 1572872 | tf_op jit(solution)/shard_map/ppermute | solution.py:514
  98.4 14.5 %collective-permute-start.20 = (bf16[256,1024]{1,0:T(8,128)(2,1)}, bf16[256,1024]{1,0:T(8,128)(2,1)}, u32[]{:S(2)}, u32[]{:S(2)}) collective-permute-start(bf16[256,1024]{1,0:T(8,128)(2,1)} %fusion.3), channel_id=1, source_target_pairs={{0,8},{1,9},{2,10},{3,11},{4,12},{5,13},{6,14},{7,15},{8,0},{9,1},... | collective-permute-start | bytes 1572872 | tf_op jit(solution)/shard_map/ppermute | solution.py:514
  106.2 6.7 %copy-start.6 = (bf16[1024,1024]{1,0:T(8,128)(2,1)S(1)}, bf16[1024,1024]{1,0:T(8,128)(2,1)}, u32[]{:S(2)}) copy-start(bf16[1024,1024]{1,0:T(8,128)(2,1)} %pad_maximum_fusion.refs_4_) | copy-start | bytes 6291460
  108.0 18.6 %collective-permute-start.13 = (bf16[2,256,640]{2,1,0:T(8,128)(2,1)}, bf16[2,256,640]{2,1,0:T(8,128)(2,1)}, u32[]{:S(2)}, u32[]{:S(2)}) collective-permute-start(bf16[2,256,640]{2,1,0:T(8,128)(2,1)} %pad_maximum_fusion.3), channel_id=1, source_target_pairs={{0,4},{1,5},{2,6},{3,7},{4,0},{5,1},{6,2},{7,3},{8,12},{9,13},{10,... | collective-permute-start | bytes 1966088 | tf_op jit(solution)/shard_map/ppermute | solution.py:514
  109.0 21.3 %collective-permute-start.11 = (bf16[2,256,640]{2,1,0:T(8,128)(2,1)}, bf16[2,256,640]{2,1,0:T(8,128)(2,1)}, u32[]{:S(2)}, u32[]{:S(2)}) collective-permute-start(bf16[2,256,640]{2,1,0:T(8,128)(2,1)} %dynamic-slice_bitcast_fusion), channel_id=1, source_target_pairs={{0,2},{1,3},{2,0},{3,1},{4,6},{5,7},{6,4},{7,5},{8,10},{9,11},{10,... | collective-permute-start | bytes 1966088 | tf_op jit(solution)/shard_map/ppermute | solution.py:514
  115.2 11.4 %copy-start.7 = (bf16[2,256,384]{2,1,0:T(8,128)(2,1)S(1)}, bf16[2,256,384]{2,1,0:T(8,128)(2,1)}, u32[]{:S(2)}) copy-start(bf16[2,256,384]{2,1,0:T(8,128)(2,1)} %get-tuple-element.71) | copy-start | bytes 1179652
  116.7 49.5 %all-to-all-start = ((bf16[32,16,1152]{2,1,0:T(8,128)(2,1)}), bf16[32,16,1152]{2,1,0:T(8,128)(2,1)S(1)}, u32[]{:S(2)}, u32[]{:S(2)}) async-start(bf16[32,16,1152]{2,1,0:T(8,128)(2,1)} %bitcast.28), calls=%async_computation | async-start | bytes 2359296 | tf_op jit(solution)/shard_map/all_to_all | solution.py:435
  127.9 16.1 %collective-permute-start.14 = (bf16[256,640]{1,0:T(8,128)(2,1)S(1)}, bf16[256,640]{1,0:T(8,128)(2,1)S(1)}, u32[]{:S(2)}, u32[]{:S(2)}) collective-permute-start(bf16[256,640]{1,0:T(8,128)(2,1)S(1)} %dynamic-slice_bitcast_fusion.3), channel_id=1, source_target_pairs={{0,2},{1,3},{2,0},{3,1},{4,6},{5,7},{6,4},{7,5},{8,10},{9,11},{10,... | collective-permute-start | bytes 983048 | tf_op jit(solution)/shard_map/ppermute | solution.py:514
  131.6 16.1 %collective-permute-start.12 = (bf16[256,640]{1,0:T(8,128)(2,1)S(1)}, bf16[256,640]{1,0:T(8,128)(2,1)S(1)}, u32[]{:S(2)}, u32[]{:S(2)}) collective-permute-start(bf16[256,640]{1,0:T(8,128)(2,1)S(1)} %dynamic-slice_bitcast_fusion.4), channel_id=1, source_target_pairs={{0,4},{1,5},{2,6},{3,7},{4,0},{5,1},{6,2},{7,3},{8,12},{9,13},{10,... | collective-permute-start | bytes 983048 | tf_op jit(solution)/shard_map/ppermute | solution.py:514
  144.2 10.7 %collective-permute-start.17 = (bf16[128,256]{1,0:T(8,128)(2,1)S(1)}, bf16[128,256]{1,0:T(8,128)(2,1)S(1)}, u32[]{:S(2)}, u32[]{:S(2)}) collective-permute-start(bf16[128,256]{1,0:T(8,128)(2,1)S(1)} %get-tuple-element.81), channel_id=1, source_target_pairs={{0,0},{1,2},{2,8},{3,10},{4,16},{5,18},{6,24},{7,26},{8,4},{9,6},{... | collective-permute-start | bytes 196616 | tf_op jit(solution)/shard_map/ppermute | solution.py:514
  144.8 10.0 %collective-permute-start.18 = (bf16[128,256]{1,0:T(8,128)(2,1)S(1)}, bf16[128,256]{1,0:T(8,128)(2,1)S(1)}, u32[]{:S(2)}, u32[]{:S(2)}) collective-permute-start(bf16[128,256]{1,0:T(8,128)(2,1)S(1)} %get-tuple-element.82), channel_id=1, source_target_pairs={{0,1},{1,3},{2,9},{3,11},{4,17},{5,19},{6,25},{7,27},{8,5},{9,7},{... | collective-permute-start | bytes 196616 | tf_op jit(solution)/shard_map/ppermute | solution.py:514
  147.9 7.6 %collective-permute-start.15 = (bf16[128,1024]{1,0:T(8,128)(2,1)S(1)}, bf16[128,1024]{1,0:T(8,128)(2,1)S(1)}, u32[]{:S(2)}, u32[]{:S(2)}) collective-permute-start(bf16[128,1024]{1,0:T(8,128)(2,1)S(1)} %get-tuple-element.77), channel_id=1, source_target_pairs={{0,0},{1,8},{2,2},{3,10},{4,4},{5,12},{6,6},{7,14},{8,16},{9,24},{... | collective-permute-start | bytes 786440 | tf_op jit(solution)/shard_map/ppermute | solution.py:514
  148.6 16.0 %collective-permute-start.16 = (bf16[128,1024]{1,0:T(8,128)(2,1)S(1)}, bf16[128,1024]{1,0:T(8,128)(2,1)S(1)}, u32[]{:S(2)}, u32[]{:S(2)}) collective-permute-start(bf16[128,1024]{1,0:T(8,128)(2,1)S(1)} %get-tuple-element.78), channel_id=1, source_target_pairs={{0,1},{1,9},{2,3},{3,11},{4,5},{5,13},{6,7},{7,15},{8,17},{9,25},{... | collective-permute-start | bytes 786440 | tf_op jit(solution)/shard_map/ppermute | solution.py:514
  165.4 6.7 %copy-start.1 = (bf16[1024,1024]{1,0:T(8,128)(2,1)S(1)}, bf16[1024,1024]{1,0:T(8,128)(2,1)}, u32[]{:S(2)}) copy-start(bf16[1024,1024]{1,0:T(8,128)(2,1)} %param.17) | copy-start | bytes 6291460
  (9 other events, 16.0 us)
